TPU v7x, 256 devices: a whole 4x4x8 slice. The times are simulated.
256 devices in a mesh: dp: 64 (over x, z, core), mp: 4 (over y).
Axes of the slice: x: 4, y: 4, z: 8, core: 2. Of those that a mesh axis runs over, the one named last changes fastest.
Arguments:
- gradient: bfloat16 [128, 1024, 1024], P('dp', 'mp'), may hold values from -3 to 3
- left_codes: bfloat16 [128, 1024, 1024], P('dp', 'mp'), may hold values from -1 to 1
- left_scales: bfloat16 [128, 1024], P('dp', 'mp'), may hold values from 0.5 to 5
- right_codes: bfloat16 [128, 1024, 1024], P('dp', 'mp'), may hold values from -1 to 1
- right_scales: bfloat16 [128, 1024], P('dp', 'mp'), may hold values from 0.5 to 5
- left_root_codes: bfloat16 [128, 1024, 1024], P('dp', 'mp'), may hold values from -0.1 to 1, as said below
- left_root_scales: bfloat16 [128, 1024], P('dp', 'mp'), may hold values from 0.5 to 2
- right_root_codes: bfloat16 [128, 1024, 1024], P('dp', 'mp'), may hold values from -0.1 to 1, as said below
- right_root_scales: bfloat16 [128, 1024], P('dp', 'mp'), may hold values from 0.5 to 2
- owner_plan: int32 [128], replicated, may hold values from 0 to 127, as said below
Outputs:
- new_left_codes: bfloat16 [128, 1024, 1024], P('dp', 'mp')
- new_left_scales: bfloat16 [128, 1024], P('dp', 'mp')
- new_right_codes: bfloat16 [128, 1024, 1024], P('dp', 'mp')
- new_right_scales: bfloat16 [128, 1024], P('dp', 'mp')
- update: bfloat16 [128, 1024, 1024], P('dp', 'mp')
Inputs may be any that keep to these rules, and one draw needn't show every extreme that they name: `left_root_codes`: each row i has one entry on the diagonal between 0.6 and 1 and small entries elsewhere. `right_root_codes`: each row i has one entry on the diagonal between 0.6 and 1 and small entries elsewhere. `owner_plan`: A permutation of the 128 slots; slot s lies on device s // 2 of dp. Exactly 12 blocks get a slot on another device; from each device at most one block leaves and at most one arrives, and an arriving block takes the slot that the device's leaving block frees; every other block keeps its slot.
All inputs are finite; a program needn't handle non-finite values. Where the computation divides by a largest or mean magnitude, that divisor is 1e-20 or more.
Results may differ from a plain program's by a relative error of at most 0.009.
Values may be sent and summed in bfloat16 or wider, within the bound.
A program may use at most 64 MiB of HBM per device.

v0:
```python
import math

import jax
import jax.numpy as jnp
from jax import lax
from jax.sharding import PartitionSpec as P

DECAY = 0.95
EPSILON = 1e-06


def side_by_side(arrays, axis, dim, along):
    widths = [math.prod(a.shape[along:]) for a in arrays]
    both = jnp.concatenate(
        [a.reshape(*a.shape[:along], w) for a, w in zip(arrays, widths)], axis=along
    )
    result = lax.all_gather(both, axis, axis=dim, tiled=True)
    tiles = jnp.split(result, [sum(widths[:k]) for k in range(1, len(widths))], axis=along)
    return tuple(
        (b.reshape(*result.shape[:along], *a.shape[along:]) for a, b in zip(arrays, tiles))
    )


def in_one_piece(arrays, axis, split_dim, concat_dim, along):
    columns = [a.reshape(*a.shape[:along], -1) for a in arrays]
    both = jnp.concatenate(columns, axis=along)
    result, at, done = (
        lax.all_to_all(both, axis, split_axis=split_dim, concat_axis=concat_dim, tiled=True),
        0,
        [],
    )
    for a, column in zip(arrays, columns):
        slab = result[..., at : at + column.shape[along]]
        done.append(slab.reshape(*slab.shape[:along], *a.shape[along:]))
        at += column.shape[along]
    return tuple(done)


def dequantize(codes, scales):
    return codes.astype(jnp.float32) * scales.astype(jnp.float32)[..., None]


def requantize(matrix):
    scales = (jnp.max(jnp.abs(matrix), axis=-1) + EPSILON).astype(jnp.bfloat16)
    codes = (matrix / scales.astype(jnp.float32)[..., None]).astype(jnp.bfloat16)
    return (codes, scales)


def refresh(
    gradient,
    left_codes,
    left_scales,
    right_codes,
    right_scales,
    left_root_codes,
    left_root_scales,
    right_root_codes,
    right_root_scales,
):
    gathered = lax.all_gather(gradient, "mp", axis=1, tiled=True)
    height = gradient.shape[1]
    offset = lax.axis_index("mp") * height
    left_new = DECAY * dequantize(left_codes, left_scales) + jnp.einsum(
        "sik,sjk->sij", gradient, gathered, preferred_element_type=jnp.float32
    )
    columns = lax.dynamic_slice_in_dim(gathered, offset, height, 2)
    right_new = DECAY * dequantize(right_codes, right_scales) + jnp.einsum(
        "sji,sjk->sik", columns, gathered, preferred_element_type=jnp.float32
    )
    left_root = dequantize(left_root_codes, left_root_scales).astype(jnp.bfloat16)
    lifted = jnp.einsum(
        "sik,skj->sij", left_root, gathered, preferred_element_type=jnp.float32
    ).astype(jnp.bfloat16)
    code_piece, scale_piece = side_by_side((right_root_codes, right_root_scales), "mp", 1, 2)
    root_piece = dequantize(code_piece, scale_piece).astype(jnp.bfloat16)
    direction = jnp.einsum("sik,skj->sij", lifted, root_piece, preferred_element_type=jnp.float32)
    grad_square = jnp.sum(jnp.square(gradient.astype(jnp.float32)), axis=(1, 2))
    dir_square = jnp.sum(jnp.square(direction), axis=(1, 2))
    grad_total, dir_total = lax.psum((grad_square, dir_square), "mp")
    scaling = jnp.sqrt(grad_total + EPSILON) / jnp.sqrt(dir_total + EPSILON)
    update = (direction * scaling[:, None, None]).astype(jnp.bfloat16)
    left_out, left_scale = requantize(left_new)
    right_out, right_scale = requantize(right_new)
    return (update, left_out, left_scale, right_out, right_scale)


def routing(owner_plan, slot_count):
    owners = lax.axis_size("dp")
    myself = lax.axis_index("dp")
    blocks = jnp.arange(owner_plan.shape[0], dtype=jnp.int32)
    anchors = blocks // slot_count
    targets = owner_plan // slot_count
    moving = anchors != targets
    leaving = moving & (anchors == myself)
    vacancy = jnp.sum(jnp.where(leaving, blocks % slot_count, 0))
    present = jnp.any(leaving)
    device_ids = jnp.arange(owners, dtype=jnp.int32)
    forward = jnp.sum(
        jnp.where(moving[:, None] & (targets[:, None] == device_ids[None, :]), anchors[:, None], 0),
        axis=0,
    )
    backward = jnp.sum(
        jnp.where(moving[:, None] & (anchors[:, None] == device_ids[None, :]), targets[:, None], 0),
        axis=0,
    )
    retain = present & (jnp.arange(slot_count, dtype=jnp.int32) == vacancy)
    return (forward[:, None], backward[:, None], vacancy, retain)


def outgoing(values, vacancy):
    return lax.dynamic_slice_in_dim(values, vacancy, 1, 0)


def landing(values, arrived, retain):
    layout = [1] * values.ndim
    layout[0] = values.shape[0]
    return jnp.where(retain.reshape(layout), arrived, values)


def spread_states(stacked, stacked_scales, chooser):
    data_parts, scale_parts = in_one_piece((stacked, stacked_scales), "dp", 2, 1, 3)
    data_back, scale_back = in_one_piece(
        (data_parts[:, chooser], scale_parts[:, chooser]), "dp", 1, 3, 4
    )
    return (data_back[:, 0], scale_back[:, 0])


def local(
    gradient,
    left_codes,
    left_scales,
    right_codes,
    right_scales,
    left_root_codes,
    left_root_scales,
    right_root_codes,
    right_root_scales,
    owner_plan,
):
    slot_count = gradient.shape[0]
    forward, backward, vacancy, retain = routing(owner_plan, slot_count)
    update, left_out, left_scale, right_out, right_scale = refresh(
        gradient,
        left_codes,
        left_scales,
        right_codes,
        right_scales,
        left_root_codes,
        left_root_scales,
        right_root_codes,
        right_root_scales,
    )
    stacked = jnp.stack([outgoing(left_out, vacancy), outgoing(right_out, vacancy)])
    stacked_scales = jnp.stack([outgoing(left_scale, vacancy), outgoing(right_scale, vacancy)])
    data_back, scale_back = spread_states(stacked, stacked_scales, forward)
    new_left = landing(left_out, data_back[0], retain)
    new_left_scale = landing(left_scale, scale_back[0], retain)
    new_right = landing(right_out, data_back[1], retain)
    new_right_scale = landing(right_scale, scale_back[1], retain)
    return (new_left, new_left_scale, new_right, new_right_scale, update)


def solution(mesh):
    placed = (
        P("dp", "mp", None),
        P("dp", "mp", None),
        P("dp", "mp"),
        P("dp", "mp", None),
        P("dp", "mp"),
        P("dp", "mp", None),
        P("dp", "mp"),
        P("dp", "mp", None),
        P("dp", "mp"),
        P(),
    )
    return jax.shard_map(
        local,
        mesh=mesh,
        in_specs=placed,
        out_specs=(
            P("dp", "mp", None),
            P("dp", "mp"),
            P("dp", "mp", None),
            P("dp", "mp"),
            P("dp", "mp", None),
        ),
        check_vma=False,
    )
```

profile of v0, /device:TPU:1, one launch (start us, length us, event | category | flops | bytes accessed | tf_op | source)
XLA Modules:
  0.0 179.1 jit_solution(12612929652434687628)
XLA Ops:
  7.2 0.0 all-gather.3.cloned.1.call-start
  7.2 0.7 all-gather.3.cloned.1.call-update
  7.9 0.0 all-gather.5.cloned.1.call-start
  8.0 0.9 copy.68
  8.8 2.3 %pad_maximum_fusion.1 = bf16[2,256,1025]{2,1,0:T(8,128)(2,1)} fusion(bf16[2,256,1]{2,1,0:T(8,128)(2,1)S(1)} %copy.68, bf16[2,256,1024]{2,1,0:T(8,128)(2,1)} %param.17), kind=kLoop, calls=%fused_computation.19 | loop fusion | flops 2099200 | bytes 2099200 | tf_op jit(solution)/shard_map/concatenate | solution.py:14
  11.2 0.0 all-gather.5.cloned.1.call-update
  11.2 0.6 fusion.10
  13.2 0.0 copy-done.4
  13.9 0.0 copy-start.2
  13.9 50.6 %all-gather.3.cloned.1.call-done = bf16[2,1024,1024]{2,1,0:T(8,128)(2,1)} async-done(((bf16[2,256,1024]{2,1,0:T(8,128)(2,1)}), bf16[2,1024,1024]{2,1,0:T(8,128)(2,1)}) %all-gather.3.cloned.1.call-update) | async-done | bytes 4194320 | tf_op jit(solution)/shard_map/all_gather | solution.py:60
  64.5 4.5 %abs_reduce_fusion = (f32[2,256]{1,0:T(2,128)S(1)}, f32[2,256,1024]{2,1,0:T(8,128)S(1)}) fusion(bf16[2,1024,1024]{2,1,0:T(8,128)(2,1)} %all-gather.3.cloned.1.call-done, s32[]{:T(128)S(6)} %select_n.72, f32[2,256]{1,0:T(2,128)S(1)} %convert_element_type.78, bf16[2,256,1024]{2,1,0:T(8,128)(2,1)} %param.13), kind=kOutput, calls=%fused_computation.11 | convolution fusion | flops 1076887040 | bytes 8392708 | tf_op jit(solution)/shard_map/sji,sjk->sik/dot_general | solution.py:67
  69.0 1.5 abs_reduce_fusion.1
  70.6 0.1 reshape.123
  70.7 0.3 divide_convert_fusion.1
  71.0 0.3 divide_convert_fusion
  71.3 0.6 copy-done
  71.9 0.1 dynamic-slice_bitcast_fusion
  72.0 0.1 pad_maximum_fusion
  72.1 2.3 %copy.60 = bf16[2,1,256,1025]{3,0,1,2:T(2,128)(2,1)} copy(bf16[2,1,256,1025]{3,2,1,0:T(8,128)(2,1)S(1)} %pad_maximum_fusion) | data formatting | bytes 2099200 | tf_op jit(solution)/shard_map/concatenate | solution.py:26
  74.4 10.7 %all-to-all-start = ((bf16[2,1,256,1025]{3,0,1,2:T(2,128)(2,1)}), bf16[2,1,256,1025]{3,0,1,2:T(2,128)(2,1)S(1)}, u32[]{:S(2)}, u32[]{:S(2)}) async-start(bf16[2,1,256,1025]{3,0,1,2:T(2,128)(2,1)} %copy.60), calls=%async_computation | async-start | bytes 2359296 | tf_op jit(solution)/shard_map/all_to_all | solution.py:28
  85.1 0.1 select_reduce_fusion
  85.2 31.2 %all-to-all-done = bf16[2,1,256,1025]{3,0,1,2:T(2,128)(2,1)S(1)} async-done(((bf16[2,1,256,1025]{3,0,1,2:T(2,128)(2,1)}), bf16[2,1,256,1025]{3,0,1,2:T(2,128)(2,1)S(1)}, u32[]{:S(2)}, u32[]{:S(2)}) %all-to-all-start) | async-done | bytes 1049632 | tf_op jit(solution)/shard_map/all_to_all | solution.py:28
  116.4 0.1 slice.39
  116.5 2.1 %slice.38 = bf16[2,64,4,1024]{3,0,2,1:T(2,128)(2,1)} slice(bf16[2,64,4,1025]{3,0,2,1:T(2,128)(2,1)S(1)} %bitcast.37), slice={[0:2], [0:64], [0:4], [0:1024]} | slice | bytes 2097152 | tf_op jit(solution)/shard_map/slice | solution.py:33
  118.7 0.1 copy.62
  118.8 2.6 %copy.74 = bf16[2,64,4,1024]{3,2,1,0:T(4,128)(2,1)} copy(bf16[2,64,4,1024]{3,0,2,1:T(2,128)(2,1)} %slice.38) | data formatting | bytes 2097152
  121.4 0.1 copy.63
  121.5 2.7 %gather_fusion = bf16[64,2,4,1024]{3,2,1,0:T(4,128)(2,1)S(1)} fusion(bf16[2,64,4,1024]{3,2,1,0:T(4,128)(2,1)} %copy.74, s32[1024]{0:T(1024)S(1)} %pad_clamp_fusion), kind=kCustom, calls=%fused_computation | custom fusion | bytes 2097408 | tf_op jit(solution)/shard_map/gather | solution.py:123
  124.2 0.6 gather_fusion.1
  124.9 0.9 copy.65
  125.7 1.7 maximum_bitcast_fusion
  127.4 6.2 %all-to-all-start.1 = ((bf16[2,64,1,4,1025]{4,3,0,2,1:T(4,128)(2,1)}), bf16[2,64,1,4,1025]{4,3,0,2,1:T(4,128)(2,1)S(1)}, u32[]{:S(2)}, u32[]{:S(2)}) async-start(bf16[2,64,1,4,1025]{4,3,0,2,1:T(4,128)(2,1)} %maximum_bitcast_fusion), calls=%async_computation.1 | async-start | bytes 2359296 | tf_op jit(solution)/shard_map/all_to_all | solution.py:28
  133.6 0.6 fusion.13
  134.2 1.3 compare_and_fusion
  135.5 1.6 multiply_reduce_fusion.1
  137.2 1.3 convert_reduce_fusion
  138.4 7.6 %multiply_reduce_fusion = (f32[2]{0:T(128)S(1)}, f32[2,256,1024]{2,1,0:T(8,128)}) fusion(bf16[2,1024,1025]{2,1,0:T(8,128)(2,1)} %all-gather.5.cloned.1.call-done, f32[2,1024]{1,0:T(2,128)S(1)} %convert_reduce_fusion, bf16[2,1024,1024]{2,1,0:T(8,128)(2,1)} %all-gather.3.cloned.1.call-done, bf16[2,256,1024]{2,1,0:T(8,128)(2,1)} %param.15, ...), kind=kOutput, calls=%fused_computation.7 | convolution fusion | flops 2156920832 | bytes 11544584 | tf_op jit(solution)/shard_map/sik,skj->sij/dot_general | solution.py:76
  146.0 7.4 %all-reduce = (f32[2]{0:T(128)S(1)}, f32[2]{0:T(128)S(1)}) all-reduce(f32[2]{0:T(128)S(1)} %get-tuple-element.25, f32[2]{0:T(128)S(1)} %multiply_reduce_fusion.1), channel_id=1, replica_groups=mesh['dp'=64,'mp'=4] {'mp'}, use_global_device_ids=true, to_apply=%region_8.9 | all-reduce | flops 4 | bytes 32 | tf_op jit(solution)/shard_map/psum | solution.py:79
  153.4 2.9 %multiply_convert_fusion.2 = bf16[2,256,1024]{2,1,0:T(8,128)(2,1)} fusion(f32[2,256,1024]{2,1,0:T(8,128)} %get-tuple-element.26, f32[2]{0:T(128)S(1)} %rsqrt_multiply_fusion), kind=kLoop, calls=%fused_computation.6 | loop fusion | flops 1048576 | bytes 3145736 | tf_op jit(solution)/shard_map/convert_element_type | solution.py:81
  156.2 8.7 %all-to-all-done.1 = bf16[2,64,1,4,1025]{4,3,0,2,1:T(4,128)(2,1)S(1)} async-done(((bf16[2,64,1,4,1025]{4,3,0,2,1:T(4,128)(2,1)}), bf16[2,64,1,4,1025]{4,3,0,2,1:T(4,128)(2,1)S(1)}, u32[]{:S(2)}, u32[]{:S(2)}) %all-to-all-start.1) | async-done | bytes 1049632 | tf_op jit(solution)/shard_map/all_to_all | solution.py:28
  164.9 0.9 copy.67
  165.9 1.1 slice_reduce_fusion
  167.0 1.5 fusion.16
  168.5 0.2 copy.77
  168.7 0.2 copy.78
  168.8 0.6 broadcast_select_fusion.2
  169.5 0.6 copy-done.1
  170.1 2.2 %broadcast_select_fusion = (bf16[2,256,1024]{2,1,0:T(8,128)(2,1)}, bf16[2,256,1024]{2,1,0:T(8,128)(2,1)}) fusion(pred[2]{0:T(512)(128)(4,1)S(1)} %compare_and_fusion, bf16[256,1024]{1,0:T(8,128)(2,1)S(1)} %bitcast.39, bf16[256,1024]{1,0:T(8,128)(2,1)S(1)} %bitcast.40, f32[2,256,1024]{2,1,0:T(8,128)S(1)} %copy-done.1, f32[2,256]{1,0:T(2,128)S(1)} %get-tuple-element.13, ...), kind=kLoop, calls=%fused_computation.23 | loop fusion | flops 3145728 | bytes 7344130 | tf_op jit(solution)/shard_map/jit(_where)/select_n | solution.py:117
  (27 shorter events, 0.1 us)
Async XLA Ops:
  7.2 57.3 %all-gather.3.cloned.1.call-start = ((), (), s32[]{:S(2)}) async-start(), calls=%async_computation.2 | async-start | bytes 5242880 | tf_op jit(solution)/shard_map/all_gather | solution.py:60
  7.9 3.3 %copy-start.8 = (s32[128]{0:T(128)S(1)}, s32[128]{0:T(128)}, u32[]{:S(2)}) copy-start(s32[128]{0:T(128)} %param.19) | copy-start | bytes 1540
  7.9 5.3 %copy-start.3 = (bf16[2,256]{1,0:T(2,128)(2,1)S(1)}, bf16[2,256]{1,0:T(2,128)(2,1)}, u32[]{:S(2)}) copy-start(bf16[2,256]{1,0:T(2,128)(2,1)} %param.12) | copy-start | bytes 3076
  7.9 5.3 %copy-start.4 = (bf16[2,256]{1,0:T(2,128)(2,1)S(1)}, bf16[2,256]{1,0:T(2,128)(2,1)}, u32[]{:S(2)}) copy-start(bf16[2,256]{1,0:T(2,128)(2,1)} %param.14) | copy-start | bytes 3076
  7.9 129.2 %all-gather.5.cloned.1.call-start = ((), (), s32[]{:S(2)}) async-start(), calls=%async_computation.3 | async-start | bytes 5898240 | tf_op jit(solution)/shard_map/all_gather | solution.py:17
  13.9 55.1 %copy-start.2 = (bf16[2,256,1024]{2,1,0:T(8,128)(2,1)S(1)}, bf16[2,256,1024]{2,1,0:T(8,128)(2,1)}, u32[]{:S(2)}) copy-start(bf16[2,256,1024]{2,1,0:T(8,128)(2,1)} %param.10) | copy-start | bytes 3145732
  64.5 4.5 %copy-start.6 = (bf16[2,1024,1024]{2,1,0:T(8,128)(2,1)S(1)}, bf16[2,1024,1024]{2,1,0:T(8,128)(2,1)}, u32[]{:S(2)}) copy-start(bf16[2,1024,1024]{2,1,0:T(8,128)(2,1)} %all-gather.3.cloned.1.call-done) | copy-start | bytes 12582916
  64.5 4.5 %copy-start.7 = (bf16[2,256,1024]{2,1,0:T(8,128)(2,1)S(1)}, bf16[2,256,1024]{2,1,0:T(8,128)(2,1)}, u32[]{:S(2)}) copy-start(bf16[2,256,1024]{2,1,0:T(8,128)(2,1)} %param.11) | copy-start | bytes 3145732
  70.5 1.4 copy-start
  74.4 42.1 %all-to-all-start = ((bf16[2,1,256,1025]{3,0,1,2:T(2,128)(2,1)}), bf16[2,1,256,1025]{3,0,1,2:T(2,128)(2,1)S(1)}, u32[]{:S(2)}, u32[]{:S(2)}) async-start(bf16[2,1,256,1025]{3,0,1,2:T(2,128)(2,1)} %copy.60), calls=%async_computation | async-start | bytes 2359296 | tf_op jit(solution)/shard_map/all_to_all | solution.py:28
  125.7 7.9 %copy-start.5 = (bf16[2,256]{1,0:T(2,128)(2,1)S(1)}, bf16[2,256]{1,0:T(2,128)(2,1)}, u32[]{:S(2)}) copy-start(bf16[2,256]{1,0:T(2,128)(2,1)} %param.16) | copy-start | bytes 3076
  127.4 37.6 %all-to-all-start.1 = ((bf16[2,64,1,4,1025]{4,3,0,2,1:T(4,128)(2,1)}), bf16[2,64,1,4,1025]{4,3,0,2,1:T(4,128)(2,1)S(1)}, u32[]{:S(2)}, u32[]{:S(2)}) async-start(bf16[2,64,1,4,1025]{4,3,0,2,1:T(4,128)(2,1)} %maximum_bitcast_fusion), calls=%async_computation.1 | async-start | bytes 2359296 | tf_op jit(solution)/shard_map/all_to_all | solution.py:28
  168.5 1.6 copy-start.1
Sparse Core Ops, SparseCore 0:
  9.8 54.5 all-gather.2
  66.3 55.5 all-gather.4
where the time goes:
time: 180 us; the launch traced here: 179 us
  waiting for transfers between devices  91.2 us (51%)
  local copies, waits for them, and re-layouts  17.7 us (10%)
  starting transfers between devices  17 us (9%)
  between operations  16.3 us (9%)
  other arithmetic  16 us (9%)
  matrix products  13.6 us (8%)
  blocking collectives  7.38 us (4%)
    all_gather x1, waiting for transfers between devices, refresh(): gathered = lax.all_gather(gradient, 'mp', axis=1, tiled=True)  50.6 us
    all_to_all x2, waiting for transfers between devices, in_one_piece(): lax.all_to_all(both, axis, split_axis=split_dim, concat_axis=concat_dim,...  39.9 us
    all_to_all x2, starting transfers between devices, in_one_piece(): lax.all_to_all(both, axis, split_axis=split_dim, concat_axis=concat_dim,...  16.9 us
    dot_general x1, matrix products, refresh(): jnp.einsum('sik,skj->sij', lifted, root_piece, preferred_element_type=jnp...  7.57 us
    psum x1, blocking collectives, refresh(): grad_total, dir_total = lax.psum((grad_square, dir_square), 'mp')  7.38 us
    dot_general x1, matrix products, refresh(): jnp.einsum('sji,sjk->sik', columns, gathered, preferred_element_type=jnp....  4.49 us
    unnamed x21, local copies, waits for them, and re-layouts  4.16 us
  transfers between devices with their start and end apart: 4, of which 3 were waited for; matrix products, arithmetic and copies ran while one was open for 22% of the time, Pallas kernels for 0%

commit v1 on v0

v1 whole, which is shorter than its diff:
```python
import functools

import jax
import jax.numpy as jnp
from jax import lax
from jax.experimental import pallas as pl
from jax.experimental.pallas import tpu as pltpu
from jax.sharding import PartitionSpec as P

DECAY = 0.95
EPSILON = 1e-06
RING = 4
HALVES = 2
MESH = pl.DeviceIdType.MESH
F32, BF16 = jnp.float32, jnp.bfloat16


def dot(a, b, dims):
    return lax.dot_general(a, b, (dims, ((), ())), preferred_element_type=F32)


def kernel(
    plan_ref, g_ref, lc_ref, ls_ref, rc_ref, rs_ref, lrc_ref, lrs_ref, rrc_ref, rrs_ref,
    nl_ref, nls_ref, nr_ref, nrs_ref, up_ref,
    ya, lroot, lifted, acc_l, acc_r, acc_f, dirs, cols, codes, scol, st, first, second, landed,
    info_v, info_s, sums_out, sums_in,
    ysend, yrecv, asend, arecv, psend, precv, isem,
):
    owners = first.shape[0]
    height, width = g_ref.shape[1:]
    half, part = height // 2, width // HALVES
    chunk = min(32, height)
    lanes = cols.shape[-1]
    piece_rows = first.shape[1]
    me, my_owner = lax.axis_index("mp"), lax.axis_index("dp")
    right, left = lax.rem(me + 1, RING), lax.rem(me + RING - 1, RING)

    barrier = pltpu.get_barrier_semaphore()
    for step in range(1, RING):
        pl.semaphore_signal(barrier, inc=1, device_id={"mp": lax.rem(me + step, RING)}, device_id_type=MESH)

    @pl.loop(1, owners)
    def _(step):
        pl.semaphore_signal(barrier, inc=1, device_id={"dp": lax.rem(my_owner + step, owners)}, device_id_type=MESH)

    blocks = plan_ref.shape[1]
    plan = jnp.transpose(jnp.broadcast_to(plan_ref[...], (blocks, blocks)))
    block = lax.broadcasted_iota(jnp.int32, (blocks, blocks), 0)
    owner = lax.broadcasted_iota(jnp.int32, (blocks, blocks), 1)
    target, anchor = lax.shift_right_logical(plan, 1), lax.shift_right_logical(block, 1)
    moving = target != anchor
    gives = moving & (anchor == owner)
    zero = jnp.zeros_like(block)
    info_v[0:1, :] = jnp.max(jnp.where(moving & (target == owner), anchor, zero), axis=0, keepdims=True)
    info_v[1:2, :] = jnp.max(jnp.where(gives, block & 1, zero), axis=0, keepdims=True)
    info_v[2:3, :] = jnp.max(jnp.where(gives, zero + 1, zero), axis=0, keepdims=True)
    to_scalars = pltpu.make_async_copy(info_v, info_s, isem)
    to_scalars.start()
    to_scalars.wait()
    vacancy, present = info_s[1, my_owner], info_s[2, my_owner] > 0
    slots = (vacancy, 1 - vacancy)

    def over_rows(body):
        @pl.loop(0, height // chunk)
        def _(r):
            body(pl.ds(pl.multiple_of(r * chunk, chunk), chunk))

    def wide(column):
        return jnp.concatenate([column] * (width // lanes), axis=1)

    for p in range(2):

        def stage(rows, p=p):
            ya[p, 0, rows, :] = g_ref[slots[p], rows, :]

        over_rows(stage)

    pl.semaphore_wait(barrier, owners - 1 + RING - 1)

    halves = (pl.ds(0, half), pl.ds(half, half))

    def hop(a, kind):
        source, target, which, to = (
            (0, 1, 0, right), (0, 1, 1, right), (0, 2, 0, left), (0, 2, 1, left), (1, 3, 0, right), (2, 3, 1, left),
        )[kind]
        return pltpu.make_async_remote_copy(
            src_ref=ya.at[a, source, halves[which]],
            dst_ref=ya.at[a, target, halves[which]],
            send_sem=ysend.at[a, kind],
            recv_sem=yrecv.at[a, kind],
            device_id={"mp": to},
            device_id_type=MESH,
        )

    def start(a, *kinds):
        for kind in kinds:
            hop(a, kind).start()

    def arrived(a, *kinds):
        for kind in kinds:
            hop(a, kind).wait_recv()

    start(0, 0, 3, 1, 2)

    for n, ref in enumerate((ls_ref, rs_ref, lrs_ref, rrs_ref)):
        both = ref[...].astype(F32)
        pair = (both[0:1, :], both[1:2, :])
        for p in range(2):
            row = jnp.where(vacancy == p, pair[0], pair[1])
            cols[n, p] = jnp.transpose(jnp.broadcast_to(row, (lanes, height)))
    for p in range(2):

        def roots(rows, p=p):
            lroot[p, rows, :] = (lrc_ref[slots[p], rows, :].astype(F32) * wide(cols[2, p, rows, :])).astype(BF16)
            ya[2 + p, 0, rows, :] = (rrc_ref[slots[p], rows, :].astype(F32) * wide(cols[3, p, rows, :])).astype(BF16)

        over_rows(roots)

    def squares(x):
        total = jnp.zeros((8, lanes), F32)
        x = jnp.sum(jnp.reshape(x * x, (x.shape[0] // 8, 8, width)), axis=0)
        for c in range(width // lanes):
            total = total + x[:, c * lanes : (c + 1) * lanes]
        return total

    for p in range(2):
        sums_out[p] = jnp.zeros((16, lanes), F32)

        def grad(rows, p=p):
            sums_out[p, 0:8, :] += squares(ya[p, 0, rows, :].astype(F32))

        over_rows(grad)

    deltas = (0, RING - 1, 1, 2)

    def columns(k):
        return pl.ds(pl.multiple_of(k * height, height), height)

    def band(p, rel):
        k = columns(lax.rem(me + deltas[rel], RING))
        acc_l[:, k] = dot(ya[p, 0], ya[p, rel], ((1,), (1,)))

        @pl.loop(0, RING)
        def _(n):
            cs = columns(n)
            x = ya[p, rel, :, cs]
            r = dot(ya[p, rel, :, columns(me)], x, ((0,), (0,)))
            f = dot(lroot[p, :, k], x, ((1,), (0,)))
            if rel == 0:
                acc_r[:, cs] = r
                acc_f[:, cs] = f
            else:
                acc_r[:, cs] += r
                acc_f[:, cs] += f

    def requantize(m, p, side, rows):
        scale = (jnp.max(jnp.abs(m), axis=1, keepdims=True) + EPSILON).astype(BF16).astype(F32)
        codes[p, side, rows, :] = (m / scale).astype(BF16)
        scol[p, side, rows, :] = jnp.broadcast_to(scale, (scale.shape[0], lanes))

    def statistics(p):
        def body(rows):
            lifted[p, rows, :] = acc_f[rows, :].astype(BF16)
            for side, (c, acc) in enumerate(((lc_ref, acc_l), (rc_ref, acc_r))):
                old = c[slots[p], rows, :].astype(F32) * wide(cols[side, p, rows, :])
                m = DECAY * old + acc[rows, :]
                if p == 0:
                    for h in range(HALVES):
                        st[h, side, rows, :] = m[:, h * part : (h + 1) * part].astype(BF16)
                requantize(m, p, side, rows)

        over_rows(body)

    pieces_down = height // piece_rows

    def piece(j):
        row = lax.div(j, HALVES)
        rows = pl.multiple_of(lax.rem(row, pieces_down) * piece_rows, piece_rows)
        return lax.rem(j, HALVES), lax.div(row, pieces_down), pl.ds(rows, piece_rows)

    mine = piece(my_owner)

    def spread(peer):
        return pltpu.make_async_remote_copy(
            src_ref=st.at[piece(peer)],
            dst_ref=first.at[my_owner],
            send_sem=asend.at[0],
            recv_sem=arecv.at[0],
            device_id={"dp": peer},
            device_id_type=MESH,
        )

    def deliver(peer):
        return pltpu.make_async_remote_copy(
            src_ref=second.at[peer],
            dst_ref=landed.at[mine],
            send_sem=asend.at[1],
            recv_sem=arecv.at[1],
            device_id={"dp": peer},
            device_id_type=MESH,
        )

    def all_but_mine(sem):
        others = first.at[pl.ds(0, owners - 1)]
        pltpu.make_async_copy(others, others, sem).wait()

    def spread_all():
        @pl.loop(1, owners)
        def _(step):
            spread(lax.rem(my_owner + step, owners)).start()

        first[my_owner] = st[mine]

    def deliver_all():
        all_but_mine(arecv.at[0])

        @pl.loop(0, owners)
        def _(d):
            second[d] = first[info_s[0, d]]

        @pl.loop(1, owners)
        def _(step):
            deliver(lax.rem(my_owner + step, owners)).start()

        landed[mine] = second[my_owner]

    def direction(p, rel):
        k = columns(lax.rem(me + deltas[rel], RING))

        @pl.loop(0, RING)
        def _(n):
            cs = columns(n)
            d = dot(lifted[p, :, k], ya[2 + p, rel, :, cs], ((1,), (0,)))
            if rel == 0:
                dirs[p, :, cs] = d
            else:
                dirs[p, :, cs] += d

    def share(p, step):
        return pltpu.make_async_remote_copy(
            src_ref=sums_out.at[p],
            dst_ref=sums_in.at[p, step - 1],
            send_sem=psend.at[p, step - 1],
            recv_sem=precv.at[p, step - 1],
            device_id={"mp": lax.rem(me + step, RING)},
            device_id_type=MESH,
        )

    def norms(p):
        def body(rows):
            sums_out[p, 8:16, :] += squares(dirs[p, rows, :])

        over_rows(body)
        for step in range(1, RING):
            share(p, step).start()

    arrived(0, 0, 3)
    start(0, 4, 5)
    band(0, 0)
    arrived(0, 1, 2)
    start(1, 0, 3, 1, 2)
    band(0, 1)
    band(0, 2)
    arrived(0, 4, 5)
    band(0, 3)
    statistics(0)
    spread_all()
    arrived(1, 0, 3)
    start(1, 4, 5)
    band(1, 0)
    arrived(1, 1, 2)
    start(2, 0, 3, 1, 2)
    band(1, 1)
    band(1, 2)
    arrived(1, 4, 5)
    band(1, 3)
    statistics(1)
    direction(0, 0)
    arrived(2, 0, 3)
    start(2, 4, 5)
    arrived(2, 1, 2)
    start(3, 0, 3, 1, 2)
    deliver_all()
    direction(0, 1)
    direction(0, 2)
    direction(1, 0)
    arrived(2, 4, 5)
    direction(0, 3)
    norms(0)
    arrived(3, 0, 3)
    start(3, 4, 5)
    arrived(3, 1, 2)
    direction(1, 1)
    direction(1, 2)
    arrived(3, 4, 5)
    direction(1, 3)
    norms(1)

    all_but_mine(arecv.at[1])

    def arriving(rows):
        for side, out in enumerate((nl_ref, nr_ref)):
            m = jnp.concatenate([landed[h, side, rows, :] for h in range(HALVES)], axis=1).astype(F32)
            scale = (jnp.max(jnp.abs(m), axis=1, keepdims=True) + EPSILON).astype(BF16).astype(F32)
            fresh = (m / scale).astype(BF16)
            first_code = jnp.where(present, fresh, codes[0, side, rows, :])
            other_code = codes[1, side, rows, :]
            out[0, rows, :] = jnp.where(vacancy == 0, first_code, other_code)
            out[1, rows, :] = jnp.where(vacancy == 0, other_code, first_code)
            scol[0, side, rows, :] = jnp.where(
                present, jnp.broadcast_to(scale, (scale.shape[0], lanes)), scol[0, side, rows, :]
            )

    over_rows(arriving)
    for side, out in enumerate((nls_ref, nrs_ref)):
        pair = [jnp.transpose(scol[p, side])[0:1, :] for p in range(2)]
        upper = jnp.where(vacancy == 0, pair[0], pair[1])
        lower = jnp.where(vacancy == 0, pair[1], pair[0])
        out[...] = jnp.concatenate([upper, lower], axis=0).astype(BF16)

    ratios = []
    for p in range(2):
        total = sums_out[p]
        for step in range(1, RING):
            share(p, step).wait_recv()
            total = total + sums_in[p, step - 1]
        grad_total = jnp.sum(total[0:8, :], keepdims=True)
        dir_total = jnp.sum(total[8:16, :], keepdims=True)
        ratios.append(jnp.sqrt(grad_total + EPSILON) / jnp.sqrt(dir_total + EPSILON))

    def grafted(rows):
        pair = [(dirs[p, rows, :] * ratios[p]).astype(BF16) for p in range(2)]
        up_ref[0, rows, :] = jnp.where(vacancy == 0, pair[0], pair[1])
        up_ref[1, rows, :] = jnp.where(vacancy == 0, pair[1], pair[0])

    over_rows(grafted)

    for a in range(4):
        for kind in range(6):
            hop(a, kind).wait_send()
    for p in range(2):
        for step in range(1, RING):
            share(p, step).wait_send()
    for phase in range(2):
        all_but_mine(asend.at[phase])


def local(*args):
    *arrays, plan = args
    slots, height, width = arrays[0].shape
    owners = lax.axis_size("dp")
    blocks = plan.shape[0]
    lanes = 128
    part = width // HALVES
    piece_rows = HALVES * 2 * height // owners
    big = jax.ShapeDtypeStruct((slots, height, width), BF16)
    small = jax.ShapeDtypeStruct((slots, height), BF16)
    vmem = pl.BlockSpec(memory_space=pltpu.VMEM)
    dma = pltpu.SemaphoreType.DMA
    return pl.pallas_call(
        kernel,
        out_shape=(big, small, big, small, big),
        in_specs=[vmem] * 10,
        out_specs=(vmem,) * 5,
        scratch_shapes=[
            pltpu.VMEM((4, RING, height, width), BF16),
            pltpu.VMEM((2, height, width), BF16),
            pltpu.VMEM((2, height, width), BF16),
            pltpu.VMEM((height, width), F32),
            pltpu.VMEM((height, width), F32),
            pltpu.VMEM((height, width), F32),
            pltpu.VMEM((2, height, width), F32),
            pltpu.VMEM((4, 2, height, lanes), F32),
            pltpu.VMEM((2, 2, height, width), BF16),
            pltpu.VMEM((2, 2, height, lanes), F32),
            pltpu.VMEM((HALVES, 2, height, part), BF16),
            pltpu.VMEM((owners, piece_rows, part), BF16),
            pltpu.VMEM((owners, piece_rows, part), BF16),
            pltpu.VMEM((HALVES, 2, height, part), BF16),
            pltpu.VMEM((8, blocks), jnp.int32),
            pltpu.SMEM((8, blocks), jnp.int32),
            pltpu.VMEM((2, 16, lanes), F32),
            pltpu.VMEM((2, RING - 1, 16, lanes), F32),
            dma((4, 6)),
            dma((4, 6)),
            dma((2,)),
            dma((2,)),
            dma((2, RING - 1)),
            dma((2, RING - 1)),
            dma,
        ],
        compiler_params=pltpu.CompilerParams(
            collective_id=0, has_side_effects=True, vmem_limit_bytes=52 * 1024 * 1024
        ),
        name="shampoo_step",
    )(plan.reshape(1, blocks), *arrays)


def solution(mesh):
    row_bands, rows = P("dp", "mp", None), P("dp", "mp")
    return jax.shard_map(
        local,
        mesh=mesh,
        in_specs=(row_bands, row_bands, rows, row_bands, rows, row_bands, rows, row_bands, rows, P()),
        out_specs=(row_bands, rows, row_bands, rows, row_bands),
        check_vma=False,
    )
```

time: 180 us -> 98.9 us (0.55)
  waiting for transfers between devices: 91.2 us -> 0 us
  Pallas kernels: 0 us -> 91.1 us
  starting transfers between devices: 17 us -> 0 us
  other arithmetic: 16 us -> 0 us
  between operations: 16.3 us -> 0.68 us
  matrix products: 13.6 us -> 0 us
  local copies, waits for them, and re-layouts: 17.7 us -> 6.88 us
  blocking collectives: 7.38 us -> 0 us
    pallas_call x0 -> x1, Pallas kernels: none -> 91.1 us  [local(): pl.pallas_call(kernel, out_shape=(big, small, big, small, big), in_specs=...]
    all_gather x2 -> x0, waiting for transfers between devices: 50.6 us -> none  [the longest x1 50.6 us: refresh(): gathered = lax.all_gather(gradient, 'mp', axis=1, tiled=True)]
    all_to_all x2 -> x0, waiting for transfers between devices: 39.9 us -> none  [in_one_piece(): lax.all_to_all(both, axis, split_axis=split_dim, concat_axis=concat_dim,...]
    all_to_all x2 -> x0, starting transfers between devices: 16.9 us -> none  [in_one_piece(): lax.all_to_all(both, axis, split_axis=split_dim, concat_axis=concat_dim,...]
    dot_general x3 -> x0, matrix products: 13.6 us -> none  [the longest x1 7.57 us: refresh(): jnp.einsum('sik,skj->sij', lifted, root_piece, preferred_element_type=jnp...]
    psum x1 -> x0, blocking collectives: 7.38 us -> none  [refresh(): grad_total, dir_total = lax.psum((grad_square, dir_square), 'mp')]
    slice x5 -> x0, local copies, waits for them, and re-layouts: 4.97 us -> none  [the longest x3 2.37 us: in_one_piece(): slab = result[..., at:at + column.shape[along]]]
    concatenate x3 -> x0, other arithmetic: 4.08 us -> none  [the longest x1 2.34 us: side_by_side(): jnp.concatenate([a.reshape(*a.shape[:along], w) for a, w in zip(arrays, w...]
  transfers between devices with their start and end apart: 4 -> 0, of which waited for: 3 -> 0; matrix products, arithmetic and copies ran while one was open for 22% -> 0% of each run, Pallas kernels for 0% -> 0%
where the time goes in v1:
time: 98.9 us; the launch traced here: 98.7 us
  Pallas kernels  91.1 us (92%)
  local copies, waits for them, and re-layouts  6.88 us (7%)
    pallas_call x1, Pallas kernels, local(): pl.pallas_call(kernel, out_shape=(big, small, big, small, big), in_specs=...  91.1 us
    unnamed x19, local copies, waits for them, and re-layouts  6.88 us

profile of v1, /device:TPU:1, one launch (start us, length us, event | category | flops | bytes accessed | tf_op | source)
XLA Modules:
  0.0 98.7 jit_solution(7610336845032908309)
XLA Ops:
  0.6 0.0 copy-start.4
  0.6 0.0 copy-start
  0.7 0.6 copy-done.4
  1.3 0.0 copy-done
  1.3 0.0 copy-start.1
  1.3 0.7 copy-done.1
  2.0 0.0 copy-start.2
  2.0 0.7 copy-done.2
  2.7 0.0 copy-start.3
  2.7 0.7 copy-done.3
  3.4 91.1 %shampoo_step.1 = (bf16[2,256,1024]{2,1,0:T(8,128)(2,1)S(1)}, bf16[2,256]{1,0:T(2,128)(2,1)S(1)}, bf16[2,256,1024]{2,1,0:T(8,128)(2,1)}, bf16[2,256]{1,0:T(2,128)(2,1)S(1)}, bf16[2,256,1024]{2,1,0:T(8,128)(2,1)}) custom-call(s32[1,128]{1,0:T(1,128)S(1)} %bitcast.1, bf16[2,256,1024]{2,1,0:T(8,128)(2,1)} %g_ref.1, bf16[2,256,1024]{2,1,0:T(8,128)(2,1)} %lc_ref.1, ...), custom_call_target="tpu_custom_call" | custom-call | tf_op jit(solution)/shard_map/shampoo_step/pallas_call | solution.py:360
  94.5 0.0 copy-start.6
  94.5 1.0 copy.20
  95.5 0.6 copy.21
  96.0 0.1 copy-done.6
  96.1 0.0 copy-start.5
  96.1 1.0 copy.22
  97.0 0.6 copy.23
  97.6 0.1 copy-done.5
  97.7 1.0 copy.24
Async XLA Ops:
  0.6 0.7 copy-start.4
  0.6 0.7 copy-start
  1.3 0.7 copy-start.1
  2.0 0.7 copy-start.2
  2.7 0.7 copy-start.3
  94.5 1.6 %copy-start.6 = (bf16[2,256,1024]{2,1,0:T(8,128)(2,1)S(1)}, bf16[2,256,1024]{2,1,0:T(8,128)(2,1)}, u32[]{:S(2)}) copy-start(bf16[2,256,1024]{2,1,0:T(8,128)(2,1)} %get-tuple-element.12) | copy-start | bytes 3145732
  96.1 1.6 %copy-start.5 = (bf16[2,256,1024]{2,1,0:T(8,128)(2,1)S(1)}, bf16[2,256,1024]{2,1,0:T(8,128)(2,1)}, u32[]{:S(2)}) copy-start(bf16[2,256,1024]{2,1,0:T(8,128)(2,1)} %get-tuple-element.14) | copy-start | bytes 3145732

commit v2 on v1

v2 whole, which is shorter than its diff:
```python
import jax
import jax.numpy as jnp
from jax import lax
from jax.experimental import pallas as pl
from jax.experimental.pallas import tpu as pltpu
from jax.sharding import PartitionSpec as P

DECAY = 0.95
EPSILON = 1e-06
RING = 4
MESH = pl.DeviceIdType.MESH
F32, BF16 = jnp.float32, jnp.bfloat16


def dot(a, b, dims):
    return lax.dot_general(a, b, (dims, ((), ())), preferred_element_type=F32)


def kernel(
    plan_hbm, g_hbm, lc_hbm, ls_hbm, rc_hbm, rs_hbm, lrc_hbm, lrs_hbm, rrc_hbm, rrs_hbm,
    nl_hbm, nls_hbm, nr_hbm, nrs_hbm, up_hbm,
    plan_ref, g_ref, lc_ref, ls_ref, rc_ref, rs_ref, lrc_ref, lrs_ref, rrc_ref, rrs_ref,
    nl_ref, nls_ref, nr_ref, nrs_ref, up_ref,
    ya, lroot, lifted, acc_l, acc_r, acc_f, dirs, cols, codes, scol, grafted, st, first, second, landed,
    info_v, info_s, sums_out, sums_in,
    ysend, yrecv, asend, arecv, psend, precv, isem, insem, outsem,
):
    owners = first.shape[0]
    height, width = g_ref.shape[1:]
    half = height // 2
    chunk = min(32, height)
    lanes = cols.shape[-1]
    groups = owners // (2 * RING)
    piece_rows = height // groups
    me, my_owner = lax.axis_index("mp"), lax.axis_index("dp")
    right, left = lax.rem(me + 1, RING), lax.rem(me + RING - 1, RING)

    def fetch(n, source, target):
        return pltpu.make_async_copy(source, target, insem.at[n])

    inputs = [
        fetch(n, *pair)
        for n, pair in enumerate(
            (
                (plan_hbm, plan_ref), (g_hbm, g_ref), (ls_hbm, ls_ref), (lc_hbm, lc_ref), (rs_hbm, rs_ref),
                (rc_hbm, rc_ref), (lrs_hbm, lrs_ref), (rrs_hbm, rrs_ref), (lrc_hbm, lrc_ref), (rrc_hbm, rrc_ref),
            )
        )
    ]
    for copy in inputs:
        copy.start()
    outputs = [
        pltpu.make_async_copy(source, target, outsem.at[n])
        for n, (source, target) in enumerate(
            ((nl_ref, nl_hbm), (nls_ref, nls_hbm), (nr_ref, nr_hbm), (nrs_ref, nrs_hbm), (up_ref, up_hbm))
        )
    ]

    barrier = pltpu.get_barrier_semaphore()
    for step in range(1, RING):
        pl.semaphore_signal(barrier, inc=1, device_id={"mp": lax.rem(me + step, RING)}, device_id_type=MESH)

    @pl.loop(1, owners)
    def _(step):
        pl.semaphore_signal(barrier, inc=1, device_id={"dp": lax.rem(my_owner + step, owners)}, device_id_type=MESH)

    inputs[0].wait()
    blocks = plan_ref.shape[1]
    plan = jnp.transpose(jnp.broadcast_to(plan_ref[...], (blocks, blocks)))
    block = lax.broadcasted_iota(jnp.int32, (blocks, blocks), 0)
    owner = lax.broadcasted_iota(jnp.int32, (blocks, blocks), 1)
    target, anchor = lax.shift_right_logical(plan, 1), lax.shift_right_logical(block, 1)
    moving = target != anchor
    gives = moving & (anchor == owner)
    zero = jnp.zeros_like(block)
    info_v[0:1, :] = jnp.max(jnp.where(moving & (target == owner), anchor, zero), axis=0, keepdims=True)
    info_v[1:2, :] = jnp.max(jnp.where(gives, block & 1, zero), axis=0, keepdims=True)
    info_v[2:3, :] = jnp.max(jnp.where(gives, zero + 1, zero), axis=0, keepdims=True)
    to_scalars = pltpu.make_async_copy(info_v, info_s, isem)
    to_scalars.start()
    to_scalars.wait()
    vacancy, present = info_s[1, my_owner], info_s[2, my_owner] > 0
    slots = (vacancy, 1 - vacancy)

    def over_rows(body):
        @pl.loop(0, height // chunk)
        def _(r):
            body(pl.ds(pl.multiple_of(r * chunk, chunk), chunk))

    def wide(column, columns=width):
        return jnp.concatenate([column] * (columns // lanes), axis=1) if columns > lanes else column[:, :columns]

    inputs[1].wait()
    for p in range(2):

        def stage(rows, p=p):
            ya[p, 0, rows, :] = g_ref[slots[p], rows, :]

        over_rows(stage)

    def scale_columns(n, ref):
        both = ref[...].astype(F32)
        pair = (both[0:1, :], both[1:2, :])
        for p in range(2):
            row = jnp.where(vacancy == p, pair[0], pair[1])
            cols[n, p] = jnp.transpose(jnp.broadcast_to(row, (lanes, height)))

    inputs[2].wait()
    scale_columns(0, ls_ref)
    inputs[3].wait()

    pl.semaphore_wait(barrier, owners - 1 + RING - 1)

    halves = (pl.ds(0, half), pl.ds(half, half))

    def hop(a, kind):
        source, target, which, to = (
            (0, 1, 0, right), (0, 1, 1, right), (0, 2, 0, left), (0, 2, 1, left), (1, 3, 0, right), (2, 3, 1, left),
        )[kind]
        return pltpu.make_async_remote_copy(
            src_ref=ya.at[a, source, halves[which]],
            dst_ref=ya.at[a, target, halves[which]],
            send_sem=ysend.at[a, kind],
            recv_sem=yrecv.at[a, kind],
            device_id={"mp": to},
            device_id_type=MESH,
        )

    def start(a, *kinds):
        for kind in kinds:
            hop(a, kind).start()

    def arrived(a, *kinds):
        for kind in kinds:
            hop(a, kind).wait_recv()

    start(0, 0, 3, 1, 2)

    deltas = (0, RING - 1, 1, 2)

    def columns(k):
        return pl.ds(pl.multiple_of(k * height, height), height)

    def piece(j):
        q = lax.div(j, 2)
        group = lax.rem(q, groups)
        tile = lax.rem(lax.div(q, groups) + group, RING)
        return lax.rem(j, 2), tile, pl.ds(pl.multiple_of(group * piece_rows, piece_rows), piece_rows)

    mine = piece(my_owner)

    def spread(side, tile):
        @pl.loop(0, groups)
        def _(step):
            group = lax.rem(lax.rem(lax.div(my_owner, 2), groups) + step, groups)
            peer = (lax.rem(tile + RING * groups - group, RING) * groups + group) * 2 + side
            source = st.at[side, tile, pl.ds(pl.multiple_of(group * piece_rows, piece_rows), piece_rows)]

            @pl.when(peer != my_owner)
            def _():
                pltpu.make_async_remote_copy(
                    src_ref=source,
                    dst_ref=first.at[my_owner],
                    send_sem=asend.at[0],
                    recv_sem=arecv.at[0],
                    device_id={"dp": peer},
                    device_id_type=MESH,
                ).start()

    def all_but_mine(sem):
        others = first.at[pl.ds(0, owners - 1)]
        pltpu.make_async_copy(others, others, sem).wait()

    def deliver_all():
        first[my_owner] = st[mine]
        all_but_mine(arecv.at[0])

        @pl.loop(0, owners)
        def _(d):
            second[d] = first[info_s[0, d]]

        @pl.loop(1, owners)
        def _(step):
            peer = lax.rem(my_owner + step, owners)
            pltpu.make_async_remote_copy(
                src_ref=second.at[peer],
                dst_ref=landed.at[mine],
                send_sem=asend.at[1],
                recv_sem=arecv.at[1],
                device_id={"dp": peer},
                device_id_type=MESH,
            ).start()

        landed[mine] = second[my_owner]

    def left_tile(p, rel):
        k = columns(lax.rem(me + deltas[rel], RING))
        tile = dot(ya[p, 0], ya[p, rel], ((1,), (1,)))
        old = lc_ref[slots[p], :, k].astype(F32) * wide(cols[0, p], height)
        m = DECAY * old + tile
        acc_l[p, :, k] = m
        if p == 0:
            st[0, rel] = m.astype(BF16)
            spread(0, rel)

    def band(p, rel):
        k = columns(lax.rem(me + deltas[rel], RING))
        both = jnp.concatenate([jnp.transpose(ya[p, rel, :, columns(me)]), lroot[p, :, k]], axis=0)

        @pl.loop(0, RING)
        def _(n):
            cs = columns(n)
            y = dot(both, ya[p, rel, :, cs], ((1,), (0,)))
            if rel == 0:
                acc_r[p, :, cs] = y[:height]
                acc_f[:, cs] = y[height:]
            else:
                acc_r[p, :, cs] += y[:height]
                acc_f[:, cs] += y[height:]

    def right_tiles(p):
        @pl.loop(0, RING)
        def _(n):
            cs = columns(n)
            m = DECAY * (rc_ref[slots[p], :, cs].astype(F32) * wide(cols[1, p], height)) + acc_r[p, :, cs]
            acc_r[p, :, cs] = m
            if p == 0:
                st[1, n] = m.astype(BF16)
                spread(1, n)

    def requantize(m):
        scale = (jnp.max(jnp.abs(m), axis=1, keepdims=True) + EPSILON).astype(BF16).astype(F32)
        return (m / scale).astype(BF16), jnp.broadcast_to(scale, (scale.shape[0], lanes))

    def finish(p):
        def body(rows):
            lifted[p, rows, :] = acc_f[rows, :].astype(BF16)
            for side, acc in enumerate((acc_l, acc_r)):
                codes[p, side, rows, :], scol[p, side, rows, :] = requantize(acc[p, rows, :])

        over_rows(body)

    def roots(p):
        def body(rows):
            lroot[p, rows, :] = (lrc_ref[slots[p], rows, :].astype(F32) * wide(cols[2, p, rows, :])).astype(BF16)
            ya[2 + p, 0, rows, :] = (rrc_ref[slots[p], rows, :].astype(F32) * wide(cols[3, p, rows, :])).astype(BF16)

        over_rows(body)

    def squares(x):
        total = jnp.zeros((8, lanes), F32)
        x = jnp.sum(jnp.reshape(x * x, (x.shape[0] // 8, 8, width)), axis=0)
        for c in range(width // lanes):
            total = total + x[:, c * lanes : (c + 1) * lanes]
        return total

    def gradient_norm(p):
        sums_out[p] = jnp.zeros((16, lanes), F32)

        def body(rows):
            sums_out[p, 0:8, :] += squares(ya[p, 0, rows, :].astype(F32))

        over_rows(body)

    def direction(p, rel):
        k = columns(lax.rem(me + deltas[rel], RING))

        @pl.loop(0, RING)
        def _(n):
            cs = columns(n)
            d = dot(lifted[p, :, k], ya[2 + p, rel, :, cs], ((1,), (0,)))
            if rel == 0:
                dirs[p, :, cs] = d
            else:
                dirs[p, :, cs] += d

    def share(p, step):
        return pltpu.make_async_remote_copy(
            src_ref=sums_out.at[p],
            dst_ref=sums_in.at[p, step - 1],
            send_sem=psend.at[p, step - 1],
            recv_sem=precv.at[p, step - 1],
            device_id={"mp": lax.rem(me + step, RING)},
            device_id_type=MESH,
        )

    def norms(p):
        def body(rows):
            sums_out[p, 8:16, :] += squares(dirs[p, rows, :])

        over_rows(body)
        for step in range(1, RING):
            share(p, step).start()

    def ratio(p):
        total = sums_out[p]
        for step in range(1, RING):
            share(p, step).wait_recv()
            total = total + sums_in[p, step - 1]
        grad_total = jnp.sum(total[0:8, :], keepdims=True)
        dir_total = jnp.sum(total[8:16, :], keepdims=True)
        return jnp.sqrt(grad_total + EPSILON) / jnp.sqrt(dir_total + EPSILON)

    def graft(p):
        r = ratio(p)

        def body(rows):
            update = (dirs[p, rows, :] * r).astype(BF16)
            if p == 0:
                grafted[rows, :] = update
            else:
                up_ref[0, rows, :] = jnp.where(vacancy == 0, grafted[rows, :], update)
                up_ref[1, rows, :] = jnp.where(vacancy == 0, update, grafted[rows, :])

        over_rows(body)

    left_tile(0, 0)
    for n in range(4, 10):
        inputs[n].wait()
    scale_columns(1, rs_ref)
    scale_columns(2, lrs_ref)
    scale_columns(3, rrs_ref)
    roots(0)
    arrived(0, 0, 3)
    start(0, 4, 5)
    band(0, 0)
    roots(1)
    gradient_norm(0)
    arrived(0, 1, 2)
    start(1, 0, 3, 1, 2)
    left_tile(0, 1)
    left_tile(0, 2)
    band(0, 1)
    band(0, 2)
    arrived(0, 4, 5)
    left_tile(0, 3)
    band(0, 3)
    right_tiles(0)
    finish(0)
    gradient_norm(1)
    left_tile(1, 0)
    band(1, 0)
    arrived(1, 0, 3)
    start(1, 4, 5)
    start(2, 0, 3, 1, 2)
    direction(0, 0)
    deliver_all()
    arrived(1, 1, 2)
    for rel in (1, 2):
        left_tile(1, rel)
        band(1, rel)
    arrived(1, 4, 5)
    left_tile(1, 3)
    band(1, 3)
    right_tiles(1)
    finish(1)
    arrived(2, 0, 3)
    start(2, 4, 5)
    start(3, 0, 3, 1, 2)
    direction(1, 0)
    arrived(2, 1, 2)
    direction(0, 1)
    direction(0, 2)
    arrived(2, 4, 5)
    direction(0, 3)
    norms(0)
    arrived(3, 0, 3)
    start(3, 4, 5)
    graft(0)

    all_but_mine(arecv.at[1])

    def arriving(rows):
        for side, out in enumerate((nl_ref, nr_ref)):
            m = [landed[side, t, rows, :].astype(F32) for t in range(RING)]
            top = jnp.maximum(jnp.maximum(jnp.abs(m[0]), jnp.abs(m[1])), jnp.maximum(jnp.abs(m[2]), jnp.abs(m[3])))
            scale = (jnp.max(top, axis=1, keepdims=True) + EPSILON).astype(BF16).astype(F32)
            for t in range(RING):
                cs = columns(lax.rem(me + deltas[t], RING)) if side == 0 else pl.ds(t * height, height)
                fresh = (m[t] / scale).astype(BF16)
                first_code = jnp.where(present, fresh, codes[0, side, rows, cs])
                other_code = codes[1, side, rows, cs]
                out[0, rows, cs] = jnp.where(vacancy == 0, first_code, other_code)
                out[1, rows, cs] = jnp.where(vacancy == 0, other_code, first_code)
            scol[0, side, rows, :] = jnp.where(
                present, jnp.broadcast_to(scale, (scale.shape[0], lanes)), scol[0, side, rows, :]
            )

    over_rows(arriving)
    for side, out in enumerate((nls_ref, nrs_ref)):
        pair = [jnp.transpose(scol[p, side])[0:1, :] for p in range(2)]
        upper = jnp.where(vacancy == 0, pair[0], pair[1])
        lower = jnp.where(vacancy == 0, pair[1], pair[0])
        out[...] = jnp.concatenate([upper, lower], axis=0).astype(BF16)
    for copy in outputs[:4]:
        copy.start()

    arrived(3, 1, 2)
    direction(1, 1)
    direction(1, 2)
    for a in range(3):
        for kind in range(6):
            hop(a, kind).wait_send()
    for phase in range(2):
        all_but_mine(asend.at[phase])
    arrived(3, 4, 5)
    direction(1, 3)
    norms(1)
    graft(1)
    outputs[4].start()

    for kind in range(6):
        hop(3, kind).wait_send()
    for p in range(2):
        for step in range(1, RING):
            share(p, step).wait_send()
    for copy in outputs:
        copy.wait()


def results_to_hbm(*refs):
    n = len(refs[:-2]) // 3
    insem, outsem = refs[-2:]
    parts = []
    for i in range(n):
        source, target, held = refs[i], refs[n + i], refs[2 * n + i]
        slices = [pl.ds(0, 1), pl.ds(1, 1)] if len(held.shape) == 3 else [pl.ds(0, held.shape[0])]
        for part in slices:
            m = len(parts)
            parts.append(
                (
                    pltpu.make_async_copy(source.at[part], held.at[part], insem.at[m]),
                    pltpu.make_async_copy(held.at[part], target.at[part], outsem.at[m]),
                )
            )
    for inward, _ in parts:
        inward.start()
    for inward, outward in parts:
        inward.wait()
        outward.start()
    for _, outward in parts:
        outward.wait()


def local(*args):
    *arrays, plan = args
    slots, height, width = arrays[0].shape
    owners = lax.axis_size("dp")
    blocks = plan.shape[0]
    lanes = 128
    piece_rows = height // (owners // (2 * RING))
    big = jax.ShapeDtypeStruct((slots, height, width), BF16)
    small = jax.ShapeDtypeStruct((slots, height), BF16)
    outs = (big, small, big, small, big)
    hbm = pl.BlockSpec(memory_space=pl.ANY)
    dma = pltpu.SemaphoreType.DMA
    held = [plan.reshape(1, blocks), *arrays]
    results = pl.pallas_call(
        kernel,
        out_shape=outs,
        in_specs=[hbm] * 10,
        out_specs=(hbm,) * 5,
        scratch_shapes=[
            *(pltpu.VMEM(x.shape, x.dtype) for x in (*held, *outs)),
            pltpu.VMEM((4, RING, height, width), BF16),
            pltpu.VMEM((2, height, width), BF16),
            pltpu.VMEM((2, height, width), BF16),
            pltpu.VMEM((2, height, width), F32),
            pltpu.VMEM((2, height, width), F32),
            pltpu.VMEM((height, width), F32),
            pltpu.VMEM((2, height, width), F32),
            pltpu.VMEM((4, 2, height, lanes), F32),
            pltpu.VMEM((2, 2, height, width), BF16),
            pltpu.VMEM((2, 2, height, lanes), F32),
            pltpu.VMEM((height, width), BF16),
            pltpu.VMEM((2, RING, height, height), BF16),
            pltpu.VMEM((owners, piece_rows, height), BF16),
            pltpu.VMEM((owners, piece_rows, height), BF16),
            pltpu.VMEM((2, RING, height, height), BF16),
            pltpu.VMEM((8, blocks), jnp.int32),
            pltpu.SMEM((8, blocks), jnp.int32),
            pltpu.VMEM((2, 16, lanes), F32),
            pltpu.VMEM((2, RING - 1, 16, lanes), F32),
            dma((4, 6)),
            dma((4, 6)),
            dma((2,)),
            dma((2,)),
            dma((2, RING - 1)),
            dma((2, RING - 1)),
            dma,
            dma((10,)),
            dma((5,)),
        ],
        compiler_params=pltpu.CompilerParams(
            collective_id=0, has_side_effects=True, vmem_limit_bytes=60 * 1024 * 1024
        ),
        name="shampoo_step",
    )(*held)
    return pl.pallas_call(
        results_to_hbm,
        out_shape=outs,
        in_specs=[hbm] * 5,
        out_specs=(hbm,) * 5,
        scratch_shapes=[*(pltpu.VMEM(x.shape, x.dtype) for x in outs), dma((8,)), dma((8,))],
        compiler_params=pltpu.CompilerParams(vmem_limit_bytes=60 * 1024 * 1024),
        name="results_to_hbm",
    )(*results)


def solution(mesh):
    row_bands, rows = P("dp", "mp", None), P("dp", "mp")
    return jax.shard_map(
        local,
        mesh=mesh,
        in_specs=(row_bands, row_bands, rows, row_bands, rows, row_bands, rows, row_bands, rows, P()),
        out_specs=(row_bands, rows, row_bands, rows, row_bands),
        check_vma=False,
    )
```

time: 98.9 us -> 91.4 us (0.924)
  local copies, waits for them, and re-layouts: 6.88 us -> 0 us
    unnamed x19 -> x0, local copies, waits for them, and re-layouts: 6.88 us -> none
    pallas_call x1 -> x2, Pallas kernels: 91.1 us -> 90.7 us  [the longest x1 87.9 us: local(): pl.pallas_call(kernel, out_shape=outs, in_specs=[hbm] * 10, out_specs=(hb...]
where the time goes in v2:
time: 91.4 us; the launch traced here: 91.3 us
  Pallas kernels  90.7 us (99%)
    pallas_call x1, Pallas kernels, local(): pl.pallas_call(kernel, out_shape=outs, in_specs=[hbm] * 10, out_specs=(hb...  87.9 us
    pallas_call x1, Pallas kernels, local(): pl.pallas_call(results_to_hbm, out_shape=outs, in_specs=[hbm] * 5, out_sp...  2.85 us

profile of v2, /device:TPU:1, one launch (start us, length us, event | category | flops | bytes accessed | tf_op | source)
XLA Modules:
  0.0 91.3 jit_solution(17865586725018750897)
XLA Ops:
  0.6 87.9 %shampoo_step.1 = (bf16[2,256,1024]{2,1,0:T(8,128)(2,1)}, bf16[2,256]{1,0:T(2,128)(2,1)}, bf16[2,256,1024]{2,1,0:T(8,128)(2,1)}, bf16[2,256]{1,0:T(2,128)(2,1)}, bf16[2,256,1024]{2,1,0:T(8,128)(2,1)}) custom-call(s32[1,128]{1,0:T(1,128)} %bitcast.1, bf16[2,256,1024]{2,1,0:T(8,128)(2,1)} %g_hbm.1, bf16[2,256,1024]{2,1,0:T(8,128)(2,1)} %lc_hbm.1, ...), custom_call_target="tpu_custom_call" | custom-call | tf_op jit(solution)/shard_map/shampoo_step/pallas_call | solution.py:458
  88.5 2.8 %results_to_hbm.1 = (bf16[2,256,1024]{2,1,0:T(8,128)(2,1)}, bf16[2,256]{1,0:T(2,128)(2,1)}, bf16[2,256,1024]{2,1,0:T(8,128)(2,1)}, bf16[2,256]{1,0:T(2,128)(2,1)}, bf16[2,256,1024]{2,1,0:T(8,128)(2,1)}) custom-call(bf16[2,256,1024]{2,1,0:T(8,128)(2,1)} %get-tuple-element.10.refs_0_, bf16[2,256]{1,0:T(2,128)(2,1)} %get-tuple-element.11.refs_1_, ...), custom_call_target="tpu_custom_call" | custom-call | tf_op jit(solution)/shard_map/results_to_hbm/pallas_call | solution.py:499

commit v3 on v2

--- a/solution.py
+++ b/solution.py
@@ -22,8 +22,8 @@
     plan_ref, g_ref, lc_ref, ls_ref, rc_ref, rs_ref, lrc_ref, lrs_ref, rrc_ref, rrs_ref,
     nl_ref, nls_ref, nr_ref, nrs_ref, up_ref,
     ya, lroot, lifted, acc_l, acc_r, acc_f, dirs, cols, codes, scol, grafted, st, first, second, landed,
-    info_v, info_s, sums_out, sums_in,
-    ysend, yrecv, asend, arecv, psend, precv, isem, insem, outsem,
+    plan_s, info_v, info_s, sums_out, sums_in,
+    ysend, yrecv, asend, arecv, psend, precv, isem, insem, outsem, word,
 ):
     owners = first.shape[0]
     height, width = g_ref.shape[1:]
@@ -42,8 +42,9 @@
         fetch(n, *pair)
         for n, pair in enumerate(
             (
-                (plan_hbm, plan_ref), (g_hbm, g_ref), (ls_hbm, ls_ref), (lc_hbm, lc_ref), (rs_hbm, rs_ref),
+                (plan_hbm, plan_s), (g_hbm, g_ref), (ls_hbm, ls_ref), (lc_hbm, lc_ref), (rs_hbm, rs_ref),
                 (rc_hbm, rc_ref), (lrs_hbm, lrs_ref), (rrs_hbm, rrs_ref), (lrc_hbm, lrc_ref), (rrc_hbm, rrc_ref),
+                (plan_hbm, plan_ref),
             )
         )
     ]
@@ -56,31 +57,45 @@
         )
     ]
 
+    core, z = lax.rem(my_owner, 2), lax.rem(lax.div(my_owner, 2), groups)
+    x = lax.div(my_owner, 2 * groups)
+
+    def owner_at(x, z, core):
+        return {"dp": (x * groups + z) * 2 + core}
+
+    beside_z = [owner_at(x, lax.rem(z + step, groups), core) for step in (1, groups - 1)] if groups > 1 else []
+    beside_x = [owner_at(lax.rem(x + step, RING), z, core) for step in range(1, RING)]
+    other_core = [owner_at(x, z, 1 - core)]
+    ring = [{"mp": lax.rem(me + step, RING)} for step in range(1, RING)]
+    near = [*ring, *beside_x, *beside_z, *other_core]
     barrier = pltpu.get_barrier_semaphore()
-    for step in range(1, RING):
-        pl.semaphore_signal(barrier, inc=1, device_id={"mp": lax.rem(me + step, RING)}, device_id_type=MESH)
-
-    @pl.loop(1, owners)
-    def _(step):
-        pl.semaphore_signal(barrier, inc=1, device_id={"dp": lax.rem(my_owner + step, owners)}, device_id_type=MESH)
+    for device in near:
+        pl.semaphore_signal(barrier, inc=1, device_id=device, device_id_type=MESH)
+    rounds = [beside_z] * 3 + [other_core, beside_x]
+
+    def tell(n):
+        for device in rounds[n]:
+            pl.semaphore_signal(word.at[n], inc=1, device_id=device, device_id_type=MESH)
+
+    def hear(n):
+        if rounds[n]:
+            pl.semaphore_wait(word.at[n], len(rounds[n]))
 
     inputs[0].wait()
-    blocks = plan_ref.shape[1]
-    plan = jnp.transpose(jnp.broadcast_to(plan_ref[...], (blocks, blocks)))
-    block = lax.broadcasted_iota(jnp.int32, (blocks, blocks), 0)
-    owner = lax.broadcasted_iota(jnp.int32, (blocks, blocks), 1)
-    target, anchor = lax.shift_right_logical(plan, 1), lax.shift_right_logical(block, 1)
-    moving = target != anchor
-    gives = moving & (anchor == owner)
-    zero = jnp.zeros_like(block)
-    info_v[0:1, :] = jnp.max(jnp.where(moving & (target == owner), anchor, zero), axis=0, keepdims=True)
-    info_v[1:2, :] = jnp.max(jnp.where(gives, block & 1, zero), axis=0, keepdims=True)
-    info_v[2:3, :] = jnp.max(jnp.where(gives, zero + 1, zero), axis=0, keepdims=True)
-    to_scalars = pltpu.make_async_copy(info_v, info_s, isem)
-    to_scalars.start()
-    to_scalars.wait()
-    vacancy, present = info_s[1, my_owner], info_s[2, my_owner] > 0
+    moves = [lax.shift_right_logical(plan_s[0, 2 * my_owner + slot], 1) != my_owner for slot in range(2)]
+    vacancy, present = jnp.where(moves[1], 1, 0), moves[0] | moves[1]
     slots = (vacancy, 1 - vacancy)
+
+    def routing():
+        inputs[10].wait()
+        blocks = plan_ref.shape[1]
+        plan = jnp.transpose(jnp.broadcast_to(plan_ref[...], (blocks, blocks)))
+        block = lax.broadcasted_iota(jnp.int32, (blocks, blocks), 0)
+        owner = lax.broadcasted_iota(jnp.int32, (blocks, blocks), 1)
+        target, anchor = lax.shift_right_logical(plan, 1), lax.shift_right_logical(block, 1)
+        arrives = (target != anchor) & (target == owner)
+        info_v[0:1, :] = jnp.max(jnp.where(arrives, anchor, jnp.zeros_like(block)), axis=0, keepdims=True)
+        pltpu.make_async_copy(info_v, info_s, isem).start()
 
     def over_rows(body):
         @pl.loop(0, height // chunk)
@@ -90,13 +105,11 @@
     def wide(column, columns=width):
         return jnp.concatenate([column] * (columns // lanes), axis=1) if columns > lanes else column[:, :columns]
 
-    inputs[1].wait()
-    for p in range(2):
-
-        def stage(rows, p=p):
+    def stage(p):
+        def body(rows):
             ya[p, 0, rows, :] = g_ref[slots[p], rows, :]
 
-        over_rows(stage)
+        over_rows(body)
 
     def scale_columns(n, ref):
         both = ref[...].astype(F32)
@@ -105,11 +118,9 @@
             row = jnp.where(vacancy == p, pair[0], pair[1])
             cols[n, p] = jnp.transpose(jnp.broadcast_to(row, (lanes, height)))
 
-    inputs[2].wait()
-    scale_columns(0, ls_ref)
-    inputs[3].wait()
-
-    pl.semaphore_wait(barrier, owners - 1 + RING - 1)
+    inputs[1].wait()
+    stage(0)
+    pl.semaphore_wait(barrier, len(near))
 
     halves = (pl.ds(0, half), pl.ds(half, half))
 
@@ -172,6 +183,7 @@
         pltpu.make_async_copy(others, others, sem).wait()
 
     def deliver_all():
+        pltpu.make_async_copy(info_v, info_s, isem).wait()
         first[my_owner] = st[mine]
         all_but_mine(arecv.at[0])
 
@@ -314,18 +326,31 @@
 
         over_rows(body)
 
-    left_tile(0, 0)
-    for n in range(4, 10):
+    tell(0)
+    stage(1)
+    for n in range(2, 10):
         inputs[n].wait()
+    scale_columns(0, ls_ref)
     scale_columns(1, rs_ref)
     scale_columns(2, lrs_ref)
+    hear(0)
+    tell(1)
     scale_columns(3, rrs_ref)
+    routing()
+    hear(1)
+    tell(2)
     roots(0)
+    hear(2)
+    tell(3)
+    gradient_norm(0)
+    hear(3)
+    tell(4)
     arrived(0, 0, 3)
     start(0, 4, 5)
+    hear(4)
+    left_tile(0, 0)
     band(0, 0)
     roots(1)
-    gradient_norm(0)
     arrived(0, 1, 2)
     start(1, 0, 3, 1, 2)
     left_tile(0, 1)
@@ -477,6 +502,7 @@
             pltpu.VMEM((owners, piece_rows, height), BF16),
             pltpu.VMEM((owners, piece_rows, height), BF16),
             pltpu.VMEM((2, RING, height, height), BF16),
+            pltpu.SMEM((1, blocks), jnp.int32),
             pltpu.VMEM((8, blocks), jnp.int32),
             pltpu.SMEM((8, blocks), jnp.int32),
             pltpu.VMEM((2, 16, lanes), F32),
@@ -488,8 +514,9 @@
             dma((2, RING - 1)),
             dma((2, RING - 1)),
             dma,
-            dma((10,)),
+            dma((11,)),
             dma((5,)),
+            pltpu.SemaphoreType.REGULAR((5,)),
         ],
         compiler_params=pltpu.CompilerParams(
             collective_id=0, has_side_effects=True, vmem_limit_bytes=60 * 1024 * 1024

time: 91.4 us -> 87 us (0.952); the launches traced: 91.3 us -> 86 us
  Pallas kernels: 90.7 us -> 85.4 us
    pallas_call x1, Pallas kernels: 87.9 us -> 82.5 us  [local(): pl.pallas_call(kernel, out_shape=outs, in_specs=[hbm] * 10, out_specs=(hb...]
where the time goes in v3:
time: 87 us; the launch traced here: 86 us
  Pallas kernels  85.4 us (98%)
    pallas_call x1, Pallas kernels, local(): pl.pallas_call(kernel, out_shape=outs, in_specs=[hbm] * 10, out_specs=(hb...  82.5 us
    pallas_call x1, Pallas kernels, local(): pl.pallas_call(results_to_hbm, out_shape=outs, in_specs=[hbm] * 5, out_sp...  2.85 us

profile of v3, /device:TPU:1, one launch (start us, length us, event | category | flops | bytes accessed | tf_op | source)
XLA Modules:
  0.0 86.0 jit_solution(13400893682380013151)
XLA Ops:
  0.6 82.5 %shampoo_step.1 = (bf16[2,256,1024]{2,1,0:T(8,128)(2,1)}, bf16[2,256]{1,0:T(2,128)(2,1)}, bf16[2,256,1024]{2,1,0:T(8,128)(2,1)}, bf16[2,256]{1,0:T(2,128)(2,1)}, bf16[2,256,1024]{2,1,0:T(8,128)(2,1)}) custom-call(s32[1,128]{1,0:T(1,128)} %bitcast.1, bf16[2,256,1024]{2,1,0:T(8,128)(2,1)} %g_hbm.1, bf16[2,256,1024]{2,1,0:T(8,128)(2,1)} %lc_hbm.1, ...), custom_call_target="tpu_custom_call" | custom-call | tf_op jit(solution)/shard_map/shampoo_step/pallas_call | solution.py:483
  83.2 2.8 %results_to_hbm.1 = (bf16[2,256,1024]{2,1,0:T(8,128)(2,1)}, bf16[2,256]{1,0:T(2,128)(2,1)}, bf16[2,256,1024]{2,1,0:T(8,128)(2,1)}, bf16[2,256]{1,0:T(2,128)(2,1)}, bf16[2,256,1024]{2,1,0:T(8,128)(2,1)}) custom-call(bf16[2,256,1024]{2,1,0:T(8,128)(2,1)} %get-tuple-element.10.refs_0_, bf16[2,256]{1,0:T(2,128)(2,1)} %get-tuple-element.11.refs_1_, ...), custom_call_target="tpu_custom_call" | custom-call | tf_op jit(solution)/shard_map/results_to_hbm/pallas_call | solution.py:526

commit v4 on v3

--- a/solution.py
+++ b/solution.py
@@ -35,6 +35,8 @@
     me, my_owner = lax.axis_index("mp"), lax.axis_index("dp")
     right, left = lax.rem(me + 1, RING), lax.rem(me + RING - 1, RING)
 
+    halves = (pl.ds(0, half), pl.ds(half, half))
+
     def fetch(n, source, target):
         return pltpu.make_async_copy(source, target, insem.at[n])
 
@@ -48,12 +50,15 @@
             )
         )
     ]
-    for copy in inputs:
-        copy.start()
+    inputs[0].start()
+    inputs[1].start()
     outputs = [
         pltpu.make_async_copy(source, target, outsem.at[n])
         for n, (source, target) in enumerate(
-            ((nl_ref, nl_hbm), (nls_ref, nls_hbm), (nr_ref, nr_hbm), (nrs_ref, nrs_hbm), (up_ref, up_hbm))
+            (
+                (nl_ref, nl_hbm), (nls_ref, nls_hbm), (nr_ref, nr_hbm), (nrs_ref, nrs_hbm),
+                *((up_ref.at[s, rows], up_hbm.at[s, rows]) for rows in halves for s in range(2)),
+            )
         )
     ]
 
@@ -63,15 +68,23 @@
     def owner_at(x, z, core):
         return {"dp": (x * groups + z) * 2 + core}
 
-    beside_z = [owner_at(x, lax.rem(z + step, groups), core) for step in (1, groups - 1)] if groups > 1 else []
+    def along_z(*steps):
+        return [owner_at(x, lax.rem(z + step, groups), core) for step in steps]
+
     beside_x = [owner_at(lax.rem(x + step, RING), z, core) for step in range(1, RING)]
     other_core = [owner_at(x, z, 1 - core)]
     ring = [{"mp": lax.rem(me + step, RING)} for step in range(1, RING)]
-    near = [*ring, *beside_x, *beside_z, *other_core]
+    below, above = (along_z(groups - 1), along_z(1)) if groups > 1 else ([], [])
+    near = [*ring, *beside_x, *other_core, *below]
     barrier = pltpu.get_barrier_semaphore()
     for device in near:
         pl.semaphore_signal(barrier, inc=1, device_id=device, device_id_type=MESH)
-    rounds = [beside_z] * 3 + [other_core, beside_x]
+    rounds, reach = [above], 1
+    while reach < groups // 2:
+        rounds.append(along_z(reach, groups - reach))
+        reach *= 2
+    rounds += [other_core, beside_x]
+    rounds = [[]] * (word.shape[0] - len(rounds)) + rounds
 
     def tell(n):
         for device in rounds[n]:
@@ -121,8 +134,6 @@
     inputs[1].wait()
     stage(0)
     pl.semaphore_wait(barrier, len(near))
-
-    halves = (pl.ds(0, half), pl.ds(half, half))
 
     def hop(a, kind):
         source, target, which, to = (
@@ -146,6 +157,8 @@
             hop(a, kind).wait_recv()
 
     start(0, 0, 3, 1, 2)
+    for copy in inputs[2:]:
+        copy.start()
 
     deltas = (0, RING - 1, 1, 2)
 
@@ -261,8 +274,8 @@
 
     def squares(x):
         total = jnp.zeros((8, lanes), F32)
-        x = jnp.sum(jnp.reshape(x * x, (x.shape[0] // 8, 8, width)), axis=0)
-        for c in range(width // lanes):
+        x = jnp.sum(jnp.reshape(x * x, (x.shape[0] // 8, 8, x.shape[1])), axis=0)
+        for c in range(max(x.shape[1] // lanes, 1)):
             total = total + x[:, c * lanes : (c + 1) * lanes]
         return total
 
@@ -284,7 +297,10 @@
             if rel == 0:
                 dirs[p, :, cs] = d
             else:
-                dirs[p, :, cs] += d
+                d = dirs[p, :, cs] + d
+                dirs[p, :, cs] = d
+            if rel == RING - 1:
+                sums_out[p, 8:16, :] += squares(d)
 
     def share(p, step):
         return pltpu.make_async_remote_copy(
@@ -297,10 +313,6 @@
         )
 
     def norms(p):
-        def body(rows):
-            sums_out[p, 8:16, :] += squares(dirs[p, rows, :])
-
-        over_rows(body)
         for step in range(1, RING):
             share(p, step).start()
 
@@ -315,48 +327,52 @@
 
     def graft(p):
         r = ratio(p)
-
-        def body(rows):
-            update = (dirs[p, rows, :] * r).astype(BF16)
-            if p == 0:
-                grafted[rows, :] = update
-            else:
-                up_ref[0, rows, :] = jnp.where(vacancy == 0, grafted[rows, :], update)
-                up_ref[1, rows, :] = jnp.where(vacancy == 0, update, grafted[rows, :])
-
-        over_rows(body)
+        for part in range(2):
+
+            @pl.loop(0, half // chunk)
+            def _(n):
+                rows = pl.ds(pl.multiple_of(part * half + n * chunk, chunk), chunk)
+                update = (dirs[p, rows, :] * r).astype(BF16)
+                if p == 0:
+                    grafted[rows, :] = update
+                else:
+                    up_ref[0, rows, :] = jnp.where(vacancy == 0, grafted[rows, :], update)
+                    up_ref[1, rows, :] = jnp.where(vacancy == 0, update, grafted[rows, :])
+
+            if p == 1:
+                for copy in outputs[4 + 2 * part : 6 + 2 * part]:
+                    copy.start()
 
     tell(0)
     stage(1)
     for n in range(2, 10):
         inputs[n].wait()
-    scale_columns(0, ls_ref)
-    scale_columns(1, rs_ref)
-    scale_columns(2, lrs_ref)
+    for n, ref in enumerate((ls_ref, rs_ref, lrs_ref)):
+        scale_columns(n, ref)
     hear(0)
     tell(1)
     scale_columns(3, rrs_ref)
-    routing()
+    roots(0)
+    arrived(0, 0, 3)
+    start(0, 4, 5)
     hear(1)
     tell(2)
-    roots(0)
+    routing()
+    band(0, 0)
     hear(2)
     tell(3)
     gradient_norm(0)
+    arrived(0, 1, 2)
+    start(1, 0, 3, 1, 2)
     hear(3)
     tell(4)
-    arrived(0, 0, 3)
-    start(0, 4, 5)
+    band(0, 1)
+    band(0, 2)
     hear(4)
     left_tile(0, 0)
-    band(0, 0)
-    roots(1)
-    arrived(0, 1, 2)
-    start(1, 0, 3, 1, 2)
     left_tile(0, 1)
     left_tile(0, 2)
-    band(0, 1)
-    band(0, 2)
+    roots(1)
     arrived(0, 4, 5)
     left_tile(0, 3)
     band(0, 3)
@@ -432,7 +448,6 @@
     direction(1, 3)
     norms(1)
     graft(1)
-    outputs[4].start()
 
     for kind in range(6):
         hop(3, kind).wait_send()
@@ -515,7 +530,7 @@
             dma((2, RING - 1)),
             dma,
             dma((11,)),
-            dma((5,)),
+            dma((8,)),
             pltpu.SemaphoreType.REGULAR((5,)),
         ],
         compiler_params=pltpu.CompilerParams(

time: 87 us -> 84.3 us (0.969); the launches traced: 86 us -> 84.2 us
  Pallas kernels: 85.4 us -> 83.6 us
    pallas_call x1, Pallas kernels: 82.5 us -> 80.7 us  [local(): pl.pallas_call(kernel, out_shape=outs, in_specs=[hbm] * 10, out_specs=(hb...]
where the time goes in v4:
time: 84.3 us; the launch traced here: 84.2 us
  Pallas kernels  83.6 us (99%)
    pallas_call x1, Pallas kernels, local(): pl.pallas_call(kernel, out_shape=outs, in_specs=[hbm] * 10, out_specs=(hb...  80.7 us
    pallas_call x1, Pallas kernels, local(): pl.pallas_call(results_to_hbm, out_shape=outs, in_specs=[hbm] * 5, out_sp...  2.85 us

profile of v4, /device:TPU:1, one launch (start us, length us, event | category | flops | bytes accessed | tf_op | source)
XLA Modules:
  0.0 84.2 jit_solution(7647801181670573686)
XLA Ops:
  0.6 80.7 %shampoo_step.1 = (bf16[2,256,1024]{2,1,0:T(8,128)(2,1)}, bf16[2,256]{1,0:T(2,128)(2,1)}, bf16[2,256,1024]{2,1,0:T(8,128)(2,1)}, bf16[2,256]{1,0:T(2,128)(2,1)}, bf16[2,256,1024]{2,1,0:T(8,128)(2,1)}) custom-call(s32[1,128]{1,0:T(1,128)} %bitcast.1, bf16[2,256,1024]{2,1,0:T(8,128)(2,1)} %g_hbm.1, bf16[2,256,1024]{2,1,0:T(8,128)(2,1)} %lc_hbm.1, ...), custom_call_target="tpu_custom_call" | custom-call | tf_op jit(solution)/shard_map/shampoo_step/pallas_call | solution.py:498
  81.4 2.8 %results_to_hbm.1 = (bf16[2,256,1024]{2,1,0:T(8,128)(2,1)}, bf16[2,256]{1,0:T(2,128)(2,1)}, bf16[2,256,1024]{2,1,0:T(8,128)(2,1)}, bf16[2,256]{1,0:T(2,128)(2,1)}, bf16[2,256,1024]{2,1,0:T(8,128)(2,1)}) custom-call(bf16[2,256,1024]{2,1,0:T(8,128)(2,1)} %get-tuple-element.10.refs_0_, bf16[2,256]{1,0:T(2,128)(2,1)} %get-tuple-element.11.refs_1_, ...), custom_call_target="tpu_custom_call" | custom-call | tf_op jit(solution)/shard_map/results_to_hbm/pallas_call | solution.py:541

commit v5 on v4

--- a/solution.py
+++ b/solution.py
@@ -16,11 +16,17 @@
     return lax.dot_general(a, b, (dims, ((), ())), preferred_element_type=F32)
 
 
+def graft_ratio(sums):
+    grad_total = jnp.sum(sums[0:8, :], keepdims=True)
+    dir_total = jnp.sum(sums[8:16, :], keepdims=True)
+    return jnp.sqrt(grad_total + EPSILON) / jnp.sqrt(dir_total + EPSILON)
+
+
 def kernel(
     plan_hbm, g_hbm, lc_hbm, ls_hbm, rc_hbm, rs_hbm, lrc_hbm, lrs_hbm, rrc_hbm, rrs_hbm,
-    nl_hbm, nls_hbm, nr_hbm, nrs_hbm, up_hbm,
+    nl_hbm, nls_hbm, nr_hbm, nrs_hbm, dir_hbm, grafted_hbm, sums_hbm,
     plan_ref, g_ref, lc_ref, ls_ref, rc_ref, rs_ref, lrc_ref, lrs_ref, rrc_ref, rrs_ref,
-    nl_ref, nls_ref, nr_ref, nrs_ref, up_ref,
+    nl_ref, nls_ref, nr_ref, nrs_ref,
     ya, lroot, lifted, acc_l, acc_r, acc_f, dirs, cols, codes, scol, grafted, st, first, second, landed,
     plan_s, info_v, info_s, sums_out, sums_in,
     ysend, yrecv, asend, arecv, psend, precv, isem, insem, outsem, word,
@@ -57,7 +63,8 @@
         for n, (source, target) in enumerate(
             (
                 (nl_ref, nl_hbm), (nls_ref, nls_hbm), (nr_ref, nr_hbm), (nrs_ref, nrs_hbm),
-                *((up_ref.at[s, rows], up_hbm.at[s, rows]) for rows in halves for s in range(2)),
+                (dirs.at[1], dir_hbm), (grafted, grafted_hbm),
+                (sums_out.at[1], sums_hbm.at[0]), (sums_in.at[1], sums_hbm.at[pl.ds(1, RING - 1)]),
             )
         )
     ]
@@ -316,32 +323,17 @@
         for step in range(1, RING):
             share(p, step).start()
 
-    def ratio(p):
-        total = sums_out[p]
+    def graft_leaving():
+        total = sums_out[0]
         for step in range(1, RING):
-            share(p, step).wait_recv()
-            total = total + sums_in[p, step - 1]
-        grad_total = jnp.sum(total[0:8, :], keepdims=True)
-        dir_total = jnp.sum(total[8:16, :], keepdims=True)
-        return jnp.sqrt(grad_total + EPSILON) / jnp.sqrt(dir_total + EPSILON)
-
-    def graft(p):
-        r = ratio(p)
-        for part in range(2):
-
-            @pl.loop(0, half // chunk)
-            def _(n):
-                rows = pl.ds(pl.multiple_of(part * half + n * chunk, chunk), chunk)
-                update = (dirs[p, rows, :] * r).astype(BF16)
-                if p == 0:
-                    grafted[rows, :] = update
-                else:
-                    up_ref[0, rows, :] = jnp.where(vacancy == 0, grafted[rows, :], update)
-                    up_ref[1, rows, :] = jnp.where(vacancy == 0, update, grafted[rows, :])
-
-            if p == 1:
-                for copy in outputs[4 + 2 * part : 6 + 2 * part]:
-                    copy.start()
+            share(0, step).wait_recv()
+            total = total + sums_in[0, step - 1]
+        r = graft_ratio(total)
+
+        def body(rows):
+            grafted[rows, :] = (dirs[0, rows, :] * r).astype(BF16)
+
+        over_rows(body)
 
     tell(0)
     stage(1)
@@ -407,7 +399,8 @@
     norms(0)
     arrived(3, 0, 3)
     start(3, 4, 5)
-    graft(0)
+    graft_leaving()
+    outputs[5].start()
 
     all_but_mine(arecv.at[1])
 
@@ -447,7 +440,11 @@
     arrived(3, 4, 5)
     direction(1, 3)
     norms(1)
-    graft(1)
+    outputs[4].start()
+    outputs[6].start()
+    for step in range(1, RING):
+        share(1, step).wait_recv()
+    outputs[7].start()
 
     for kind in range(6):
         hop(3, kind).wait_send()
@@ -458,28 +455,71 @@
         copy.wait()
 
 
-def results_to_hbm(*refs):
-    n = len(refs[:-2]) // 3
-    insem, outsem = refs[-2:]
-    parts = []
-    for i in range(n):
-        source, target, held = refs[i], refs[n + i], refs[2 * n + i]
-        slices = [pl.ds(0, 1), pl.ds(1, 1)] if len(held.shape) == 3 else [pl.ds(0, held.shape[0])]
-        for part in slices:
-            m = len(parts)
-            parts.append(
-                (
-                    pltpu.make_async_copy(source.at[part], held.at[part], insem.at[m]),
-                    pltpu.make_async_copy(held.at[part], target.at[part], outsem.at[m]),
-                )
+def results_to_hbm(
+    plan_hbm, nl_in, nls_in, nr_in, nrs_in, dir_in, grafted_in, sums_in,
+    nl_out, nls_out, nr_out, nrs_out, up_out,
+    plan_s, nl, nls, nr, nrs, direction, grafted, sums, up,
+    insem, outsem,
+):
+    height = direction.shape[0]
+    half, chunk = height // 2, min(32, height // 2)
+    halves = (pl.ds(0, half), pl.ds(half, half))
+    inward = [
+        pltpu.make_async_copy(source, target, insem.at[n])
+        for n, (source, target) in enumerate(
+            (
+                (plan_hbm, plan_s), (sums_in, sums),
+                (dir_in.at[halves[0]], direction.at[halves[0]]), (grafted_in, grafted),
+                (dir_in.at[halves[1]], direction.at[halves[1]]),
+                (nl_in.at[0], nl.at[0]), (nl_in.at[1], nl.at[1]), (nr_in.at[0], nr.at[0]), (nr_in.at[1], nr.at[1]),
+                (nls_in, nls), (nrs_in, nrs),
             )
-    for inward, _ in parts:
-        inward.start()
-    for inward, outward in parts:
-        inward.wait()
-        outward.start()
-    for _, outward in parts:
-        outward.wait()
+        )
+    ]
+    outward = [
+        pltpu.make_async_copy(source, target, outsem.at[n])
+        for n, (source, target) in enumerate(
+            (
+                *((up.at[slot, rows], up_out.at[slot, rows]) for rows in halves for slot in range(2)),
+                (nl.at[0], nl_out.at[0]), (nl.at[1], nl_out.at[1]), (nr.at[0], nr_out.at[0]), (nr.at[1], nr_out.at[1]),
+                (nls, nls_out), (nrs, nrs_out),
+            )
+        )
+    ]
+    for copy in inward:
+        copy.start()
+    inward[0].wait()
+    my_owner = lax.axis_index("dp")
+    first_is_0 = lax.shift_right_logical(plan_s[0, 2 * my_owner + 1], 1) == my_owner
+    inward[1].wait()
+    ratio = graft_ratio((sums[0] + sums[1]) + (sums[2] + sums[3]))
+
+    def graft(part):
+        @pl.loop(0, half // chunk)
+        def _(n):
+            rows = pl.ds(pl.multiple_of(part * half + n * chunk, chunk), chunk)
+            update, leaving = (direction[rows, :] * ratio).astype(BF16), grafted[rows, :]
+            up[0, rows, :] = jnp.where(first_is_0, leaving, update)
+            up[1, rows, :] = jnp.where(first_is_0, update, leaving)
+
+    def on(first, last):
+        for n in range(first, last):
+            inward[n + 1].wait()
+            outward[n].start()
+
+    inward[2].wait()
+    inward[3].wait()
+    graft(0)
+    outward[0].start()
+    outward[1].start()
+    on(4, 6)
+    inward[4].wait()
+    graft(1)
+    outward[2].start()
+    outward[3].start()
+    on(6, 10)
+    for copy in outward:
+        copy.wait()
 
 
 def local(*args):
@@ -492,16 +532,22 @@
     big = jax.ShapeDtypeStruct((slots, height, width), BF16)
     small = jax.ShapeDtypeStruct((slots, height), BF16)
     outs = (big, small, big, small, big)
+    between = (
+        *outs[:4],
+        jax.ShapeDtypeStruct((height, width), F32),
+        jax.ShapeDtypeStruct((height, width), BF16),
+        jax.ShapeDtypeStruct((RING, 16, lanes), F32),
+    )
     hbm = pl.BlockSpec(memory_space=pl.ANY)
     dma = pltpu.SemaphoreType.DMA
     held = [plan.reshape(1, blocks), *arrays]
     results = pl.pallas_call(
         kernel,
-        out_shape=outs,
+        out_shape=between,
         in_specs=[hbm] * 10,
-        out_specs=(hbm,) * 5,
+        out_specs=(hbm,) * 7,
         scratch_shapes=[
-            *(pltpu.VMEM(x.shape, x.dtype) for x in (*held, *outs)),
+            *(pltpu.VMEM(x.shape, x.dtype) for x in (*held, *outs[:4])),
             pltpu.VMEM((4, RING, height, width), BF16),
             pltpu.VMEM((2, height, width), BF16),
             pltpu.VMEM((2, height, width), BF16),
@@ -541,12 +587,17 @@
     return pl.pallas_call(
         results_to_hbm,
         out_shape=outs,
-        in_specs=[hbm] * 5,
+        in_specs=[hbm] * 8,
         out_specs=(hbm,) * 5,
-        scratch_shapes=[*(pltpu.VMEM(x.shape, x.dtype) for x in outs), dma((8,)), dma((8,))],
+        scratch_shapes=[
+            pltpu.SMEM((1, blocks), jnp.int32),
+            *(pltpu.VMEM(x.shape, x.dtype) for x in (*between, big)),
+            dma((11,)),
+            dma((10,)),
+        ],
         compiler_params=pltpu.CompilerParams(vmem_limit_bytes=60 * 1024 * 1024),
         name="results_to_hbm",
-    )(*results)
+    )(held[0], *results)
 
 
 def solution(mesh):

time: 84.3 us -> 84.1 us (level)
  no operation moved by 1% of the time
where the time goes in v5:
time: 84.1 us; the launch traced here: 84 us
  Pallas kernels  83.3 us (99%)
    pallas_call x1, Pallas kernels, local(): pl.pallas_call(kernel, out_shape=between, in_specs=[hbm] * 10, out_specs=...  80.1 us
    pallas_call x1, Pallas kernels, local(): pl.pallas_call(results_to_hbm, out_shape=outs, in_specs=[hbm] * 8, out_sp...  3.21 us

profile of v5, /device:TPU:1, one launch (start us, length us, event | category | flops | bytes accessed | tf_op | source)
XLA Modules:
  0.0 84.0 jit_solution(1778489117429465499)
XLA Ops:
  0.6 80.1 %shampoo_step.1 = (bf16[2,256,1024]{2,1,0:T(8,128)(2,1)}, bf16[2,256]{1,0:T(2,128)(2,1)}, bf16[2,256,1024]{2,1,0:T(8,128)(2,1)}, bf16[2,256]{1,0:T(2,128)(2,1)},...) custom-call(s32[1,128]{1,0:T(1,128)} %bitcast.1, bf16[2,256,1024]{2,1,0:T(8,128)(2,1)} %g_hbm.1, ...), custom_call_target="tpu_custom_call" | custom-call | tf_op jit(solution)/shard_map/shampoo_step/pallas_call | solution.py:544
  80.8 3.2 %results_to_hbm.1 = (bf16[2,256,1024]{2,1,0:T(8,128)(2,1)}, bf16[2,256]{1,0:T(2,128)(2,1)}, bf16[2,256,1024]{2,1,0:T(8,128)(2,1)}, bf16[2,256]{1,0:T(2,128)(2,1)}, bf16[2,256,1024]{2,1,0:T(8,128)(2,1)}) custom-call(s32[1,128]{1,0:T(1,128)} %bitcast.2, bf16[2,256,1024]{2,1,0:T(8,128)(2,1)} %get-tuple-element.12.nl_in, ...), custom_call_target="tpu_custom_call" | custom-call | tf_op jit(solution)/shard_map/results_to_hbm/pallas_call | solution.py:587

commit v6 on v5

--- a/solution.py
+++ b/solution.py
@@ -81,12 +81,29 @@
     beside_x = [owner_at(lax.rem(x + step, RING), z, core) for step in range(1, RING)]
     other_core = [owner_at(x, z, 1 - core)]
     ring = [{"mp": lax.rem(me + step, RING)} for step in range(1, RING)]
-    below, above = (along_z(groups - 1), along_z(1)) if groups > 1 else ([], [])
-    near = [*ring, *beside_x, *other_core, *below]
+    near = [*ring, *beside_x, *other_core]
     barrier = pltpu.get_barrier_semaphore()
+
+    def signal(semaphore, device):
+        pl.semaphore_signal(semaphore, inc=1, device_id=device, device_id_type=MESH)
+
     for device in near:
-        pl.semaphore_signal(barrier, inc=1, device_id=device, device_id_type=MESH)
-    rounds, reach = [above], 1
+        signal(barrier, device)
+    near_count = len(near)
+    lowest, highest = z == 0, z == groups - 1
+    if groups > 2:
+        [below], [above] = along_z(groups - 1), along_z(1)
+        near_count = near_count + jnp.where(lowest, 0, jnp.where(highest, 2, 1))
+
+        @pl.when(z < groups - 1)
+        def _():
+            signal(barrier, above)
+
+        @pl.when(lowest)
+        def _():
+            signal(barrier, below)
+
+    rounds, reach = [[]], 1
     while reach < groups // 2:
         rounds.append(along_z(reach, groups - reach))
         reach *= 2
@@ -95,11 +112,25 @@
 
     def tell(n):
         for device in rounds[n]:
-            pl.semaphore_signal(word.at[n], inc=1, device_id=device, device_id_type=MESH)
+            signal(word.at[n], device)
+        if n == 0 and groups > 2:
+
+            @pl.when(z > 0)
+            def _():
+                signal(word.at[n], below)
+
+            @pl.when(highest)
+            def _():
+                signal(word.at[n], above)
 
     def hear(n):
         if rounds[n]:
             pl.semaphore_wait(word.at[n], len(rounds[n]))
+        if n == 0 and groups > 2:
+
+            @pl.when(z < groups - 1)
+            def _():
+                pl.semaphore_wait(word.at[n], jnp.where(lowest, 2, 1))
 
     inputs[0].wait()
     moves = [lax.shift_right_logical(plan_s[0, 2 * my_owner + slot], 1) != my_owner for slot in range(2)]
@@ -140,7 +171,7 @@
 
     inputs[1].wait()
     stage(0)
-    pl.semaphore_wait(barrier, len(near))
+    pl.semaphore_wait(barrier, near_count)
 
     def hop(a, kind):
         source, target, which, to = (
@@ -339,43 +370,42 @@
     stage(1)
     for n in range(2, 10):
         inputs[n].wait()
-    for n, ref in enumerate((ls_ref, rs_ref, lrs_ref)):
-        scale_columns(n, ref)
     hear(0)
     tell(1)
-    scale_columns(3, rrs_ref)
+    for n, ref in enumerate((ls_ref, rs_ref, lrs_ref, rrs_ref)):
+        scale_columns(n, ref)
+    hear(1)
+    tell(2)
     roots(0)
+    hear(2)
+    tell(3)
     arrived(0, 0, 3)
     start(0, 4, 5)
-    hear(1)
-    tell(2)
+    hear(3)
+    tell(4)
     routing()
     band(0, 0)
-    hear(2)
-    tell(3)
     gradient_norm(0)
     arrived(0, 1, 2)
     start(1, 0, 3, 1, 2)
-    hear(3)
-    tell(4)
-    band(0, 1)
-    band(0, 2)
     hear(4)
     left_tile(0, 0)
     left_tile(0, 1)
     left_tile(0, 2)
+    band(0, 1)
+    band(0, 2)
     roots(1)
     arrived(0, 4, 5)
     left_tile(0, 3)
     band(0, 3)
     right_tiles(0)
+    arrived(1, 0, 3)
+    start(1, 4, 5)
+    start(2, 0, 3, 1, 2)
     finish(0)
     gradient_norm(1)
     left_tile(1, 0)
     band(1, 0)
-    arrived(1, 0, 3)
-    start(1, 4, 5)
-    start(2, 0, 3, 1, 2)
     direction(0, 0)
     deliver_all()
     arrived(1, 1, 2)

time: 84.1 us -> 83.8 us (level)
  no operation moved by 1% of the time
where the time goes in v6:
time: 83.8 us; the launch traced here: 83.2 us
  Pallas kernels  82.5 us (98%)
    pallas_call x1, Pallas kernels, local(): pl.pallas_call(kernel, out_shape=between, in_specs=[hbm] * 10, out_specs=...  79.3 us
    pallas_call x1, Pallas kernels, local(): pl.pallas_call(results_to_hbm, out_shape=outs, in_specs=[hbm] * 8, out_sp...  3.21 us

profile of v6, /device:TPU:1, one launch (start us, length us, event | category | flops | bytes accessed | tf_op | source)
XLA Modules:
  0.0 83.2 jit_solution(5009270867871731313)
XLA Ops:
  0.6 79.3 %shampoo_step.1 = (bf16[2,256,1024]{2,1,0:T(8,128)(2,1)}, bf16[2,256]{1,0:T(2,128)(2,1)}, bf16[2,256,1024]{2,1,0:T(8,128)(2,1)}, bf16[2,256]{1,0:T(2,128)(2,1)},...) custom-call(s32[1,128]{1,0:T(1,128)} %bitcast.1, bf16[2,256,1024]{2,1,0:T(8,128)(2,1)} %g_hbm.1, ...), custom_call_target="tpu_custom_call" | custom-call | tf_op jit(solution)/shard_map/shampoo_step/pallas_call | solution.py:574
  79.9 3.2 %results_to_hbm.1 = (bf16[2,256,1024]{2,1,0:T(8,128)(2,1)}, bf16[2,256]{1,0:T(2,128)(2,1)}, bf16[2,256,1024]{2,1,0:T(8,128)(2,1)}, bf16[2,256]{1,0:T(2,128)(2,1)}, bf16[2,256,1024]{2,1,0:T(8,128)(2,1)}) custom-call(s32[1,128]{1,0:T(1,128)} %bitcast.2, bf16[2,256,1024]{2,1,0:T(8,128)(2,1)} %get-tuple-element.12.nl_in, ...), custom_call_target="tpu_custom_call" | custom-call | tf_op jit(solution)/shard_map/results_to_hbm/pallas_call | solution.py:617
